TPU v7x, 256 devices: a whole 4x4x8 slice. The times are simulated.
256 devices in a mesh: dp: 32 (over z_lo, y, core), fsdp: 8 (over z_hi, x).
Axes of the slice: x: 4, y: 4, z: 8 (z_hi: 2, z_lo: 4; z = z_hi * 4 + z_lo), core: 2. Of those that a mesh axis runs over, the one named last changes fastest.
Arguments:
- clip: bfloat16 [1, 128, 256, 1024], P(None, 'dp', 'fsdp'), may hold values from -6 to 6
- space_gain: float32 [1024], replicated, may hold values from 0.5 to 1.5
- space_qkv: bfloat16 [1024, 3072], P('fsdp'), may hold values from -2 to 2
- space_out: bfloat16 [1024, 1024], P('fsdp'), may hold values from -0.1875 to 0.1875
- mlp_gain: float32 [1024], replicated, may hold values from 0.5 to 1.5
- mlp_up: bfloat16 [1024, 4096], P('fsdp'), may hold values from -0.1875 to 0.1875
- mlp_down: bfloat16 [4096, 1024], P('fsdp'), may hold values from -0.09375 to 0.09375
- time_gain: float32 [1024], replicated, may hold values from 0.5 to 1.5
- time_qkv: bfloat16 [1024, 3072], P('fsdp'), may hold values from -2 to 2
- time_out: bfloat16 [1024, 1024], P('fsdp'), may hold values from -0.1875 to 0.1875
Outputs:
- encoded: bfloat16 [1, 128, 256, 1024], P(None, 'dp', 'fsdp')
All inputs are finite; a program needn't handle non-finite values.
Results may differ from a plain program's by a relative error of at most 0.017.
Values may be sent and summed in bfloat16 or wider, within the bound.
No kernel may reach another device: no remote copies, remote signals or barrier semaphores. Data moves between devices by JAX's collectives and lax.ppermute only.
A program may use at most 128 MiB of HBM per device.

v0:
```python
import functools

import jax
import jax.numpy as jnp
from jax import lax
from jax.experimental import pallas as pl
from jax.experimental.pallas import tpu as pltpu
from jax.sharding import PartitionSpec as P

BF = jnp.bfloat16
F32 = jnp.float32
AXES = ("dp", "fsdp")
ROWS = 128
HALF = 512
VMEM = pl.BlockSpec(memory_space=pltpu.VMEM)
SMEM = pl.BlockSpec(memory_space=pltpu.SMEM)
ANY = pl.BlockSpec(memory_space=pl.ANY)
BIG = pltpu.CompilerParams(vmem_limit_bytes=56 * 1024 * 1024)


def device(x, y, z, c):
    return (((z % 4) * 4 + y) * 2 + c) * 8 + (z // 4) * 4 + x


def chips():
    return [(x, y, z, c) for x in range(4) for y in range(4) for z in range(8) for c in range(2)]


def shift(v, x=0, y=0, z=0, c=0):
    pairs = [
        (device(a, b, d, e), device((a + x) % 4, (b + y) % 4, (d + z) % 8, (e + c) % 2)) for a, b, d, e in chips()
    ]
    return lax.ppermute(v, AXES, pairs)


def swap_chips(v):
    return lax.ppermute(v, AXES, [(device(a, b, d, e), device(a, b ^ 1, d, e)) for a, b, d, e in chips()])


def norm_rows(wide, gain):
    centre = jnp.mean(wide, axis=-1, keepdims=True)
    off = wide - centre
    spread = jnp.mean(off * off, axis=-1, keepdims=True)
    return (off * lax.rsqrt(spread + 1e-06) * gain).astype(BF)


def start_copies(pairs, sems):
    copies = []
    for i, (src, dst) in enumerate(pairs):
        copy = pltpu.make_async_copy(src, dst, sems.at[i])
        copy.start()
        copies.append(copy)
    return copies


def aligned(offset, size, unit):
    return pl.ds(pl.multiple_of(offset, unit), size)


def shares_kernel(place, sqkv, sproject, up, down, tqkv, tproject, near, reach,
                  sheads, srows, ups, downs, theads, trows, sems):
    y, c, zl, quarter = place[2], place[3], place[4], place[5]
    half = aligned(c * 64, 64, 64)
    pairs = [(sqkv, sheads), (sproject.at[half], srows)]
    for i in range(2):
        pairs.append((up.at[:, aligned((2 * zl + i) * 512 + quarter * 128, 128, 128)], ups.at[i]))
    pairs.append((down.at[aligned(quarter * 128 + zl * 32, 32, 32)], downs))
    for part in range(3):
        pairs.append((tqkv.at[:, aligned(part * 1024 + y * 256, 256, 256)], theads.at[part]))
    pairs.append((tproject.at[half, aligned(y * 256, 256, 256)], trows))
    for copy in start_copies(pairs, sems):
        copy.wait()

    source = lax.broadcasted_iota(jnp.int32, (512, 128), 0)
    lane = lax.broadcasted_iota(jnp.int32, (512, 128), 1)
    pick = (source == lane + jnp.where(lane < 64, 0, 192) + quarter * 64).astype(F32).astype(BF)
    for pair in range(2):
        at = pair * 128
        for part in range(3):
            block = sheads[:, part * 1024 + pair * 512 : part * 1024 + pair * 512 + 512]
            got = jnp.dot(block, pick, preferred_element_type=F32).astype(BF)
            for ref in (near, reach):
                ref[at : at + 128, part * 128 : part * 128 + 128] = got
        for ref in (near, reach):
            ref[at : at + 64, 384:512] = srows[:, pair * 256 : pair * 256 + 128]
            ref[at + 64 : at + 128, 384:512] = srows[:, pair * 256 + 128 : pair * 256 + 256]
    for ref in (near, reach):
        ref[256:320, :] = srows[:, 512:]
    for i in range(2):
        near[320:448, i * 128 : i * 128 + 128] = ups[i]
    for i in range(4):
        near[320 + i * 32 : 352 + i * 32, 256:512] = downs[:, i * 256 : i * 256 + 256]

    source = lax.broadcasted_iota(jnp.int32, (256, 128), 0)
    lane = lax.broadcasted_iota(jnp.int32, (256, 128), 1)
    pick = (source == lane + jnp.where(lane < 64, 0, 64) + c * 64).astype(F32).astype(BF)
    for part in range(3):
        reach[320:448, part * 128 : part * 128 + 128] = jnp.dot(theads[part], pick, preferred_element_type=F32).astype(BF)
    reach[320:384, 384:512] = trows[:, :128]
    reach[384:448, 384:512] = trows[:, 128:]


def make_shares(place, *weights):
    return pl.pallas_call(
        shares_kernel,
        out_shape=[jax.ShapeDtypeStruct((rows, HALF), BF) for rows in (448, 448)],
        in_specs=[SMEM] + [ANY] * 6,
        out_specs=[VMEM] * 2,
        scratch_shapes=[
            pltpu.VMEM((128, 3072), BF),
            pltpu.VMEM((64, 1024), BF),
            pltpu.VMEM((2, 128, 128), BF),
            pltpu.VMEM((32, 1024), BF),
            pltpu.VMEM((3, 128, 256), BF),
            pltpu.VMEM((64, 256), BF),
            pltpu.SemaphoreType.DMA((9,)),
        ],
        compiler_params=BIG,
        cost_estimate=pl.CostEstimate(flops=120000000, bytes_accessed=2500000, transcendentals=0),
    )(place, *weights)


def stack_kernel(a, b, c, d, out, sems):
    for copy in start_copies([(ref.at[pl.ds(320, 128)], out.at[pl.ds(i * 128, 128)]) for i, ref in enumerate((a, b, c, d))], sems):
        copy.wait()


def stack(pieces):
    return pl.pallas_call(
        stack_kernel,
        out_shape=jax.ShapeDtypeStruct((512, HALF), BF),
        in_specs=[ANY] * 4,
        out_specs=VMEM,
        scratch_shapes=[pltpu.SemaphoreType.DMA((4,))],
        compiler_params=BIG,
        cost_estimate=pl.CostEstimate(flops=0, bytes_accessed=1000000, transcendentals=0),
    )(*pieces)


def attend_pair(query, keys, values, seqs):
    count = query.shape[0]
    low = lax.broadcasted_iota(jnp.int32, (count, 128), 1) < 64
    mixed = []
    for mask in (low, jnp.logical_not(low)):
        one = jnp.where(mask, query, jnp.zeros_like(query))
        scores = lax.dot_general(one, keys, (((1,), (1,)), ((), ())), preferred_element_type=F32)
        if seqs > 1:
            length = count // seqs
            row = lax.broadcasted_iota(jnp.int32, (count, count), 0) // length
            column = lax.broadcasted_iota(jnp.int32, (count, count), 1) // length
            scores = jnp.where(row == column, scores, -1e30)
        weights = jnp.exp(scores - jnp.max(scores, axis=-1, keepdims=True))
        total = jnp.sum(weights, axis=-1, keepdims=True)
        mixed.append(jnp.dot(weights.astype(BF), values, preferred_element_type=F32) * (1.0 / total))
    return jnp.where(low, mixed[0], mixed[1]).astype(BF)


def space_kernel(place, own, other, far, far_other, gain, *refs):
    pieces = refs[:8]
    base, away, over, tokens, wqkv, wout, packed, att, sems = refs[8:]
    blocks = [
        (lax.rem(place[1] + step // 4, 2) * 4 + lax.rem(place[0] + step, 4), ref) for step, ref in enumerate(pieces)
    ]
    pairs = []
    for pair in range(2):
        for block, ref in blocks:
            pairs.append((ref.at[pl.ds(pair * 128, 128), pl.ds(0, 384)],
                          wqkv.at[aligned(block * 128, 128, 128), pl.ds(pair * 384, 384)]))
    copies = start_copies(pairs, sems)
    odd = lax.rem(place[0] + place[2], 2)
    late = []
    for slot in range(4):
        ways = []
        for parity in range(2):
            block, ref = blocks[(slot // 2) * 4 + (slot % 2) * 2 + parity]
            row = aligned(lax.div(block, 2) * 64, 64, 64)
            ways.append([
                pltpu.make_async_copy(src, wout.at[row, pl.ds(column, src.shape[1])], sems.at[16 + slot * 5 + i])
                for i, (src, column) in enumerate(
                    [(ref.at[pl.ds(256, 64), :], 512)]
                    + [(ref.at[pl.ds(k * 64, 64), pl.ds(384, 128)], k * 128) for k in range(4)])
            ])
        for parity in range(2):

            @pl.when(odd == parity)
            def _():
                for copy in ways[parity]:
                    copy.start()

        late.append(ways)
    for i, ref in enumerate((own, other, far, far_other)):
        tokens[i * ROWS : (i + 1) * ROWS, :] = norm_rows(ref[...].astype(F32), gain[...])
    for pair in range(2):
        for copy in copies[pair * 8 : pair * 8 + 8]:
            copy.wait()
        cols = slice(pair * 384, pair * 384 + 384)
        packed[:, cols] = jnp.dot(tokens[...], wqkv[:, cols], preferred_element_type=F32).astype(BF)
        for frame in range(2):
            rows = slice(frame * 256, frame * 256 + 256)
            query, keys, values = (packed[rows, pair * 384 + i * 128 : pair * 384 + i * 128 + 128] for i in range(3))
            att[rows, pair * 128 : pair * 128 + 128] = attend_pair(query * 0.125, keys, values, 1)
    for ways in late:
        for parity in range(2):

            @pl.when(odd == parity)
            def _():
                for copy in ways[parity]:
                    copy.wait()

    row = lambda i: jnp.dot(att[i * ROWS : (i + 1) * ROWS, :], wout[...], preferred_element_type=F32)
    away[:ROWS, :] = row(1).astype(BF)
    away[ROWS:, :] = row(3).astype(BF)
    over[...] = row(2)
    base[...] = own[...].astype(F32) + row(0)


def wide(rows, dtype=F32):
    return jax.ShapeDtypeStruct((rows, 1024), dtype)


def space_call(place, tokens, gain, pieces):
    return pl.pallas_call(
        space_kernel,
        out_shape=[wide(ROWS), wide(2 * ROWS, BF), wide(ROWS)],
        in_specs=[SMEM] + [VMEM] * 5 + [ANY] * 8,
        out_specs=[VMEM] * 3,
        scratch_shapes=[
            pltpu.VMEM((4 * ROWS, 1024), BF),
            pltpu.VMEM((1024, 768), BF),
            pltpu.VMEM((256, 1024), BF),
            pltpu.VMEM((4 * ROWS, 768), BF),
            pltpu.VMEM((4 * ROWS, 256), BF),
            pltpu.SemaphoreType.DMA((36,)),
        ],
        compiler_params=BIG,
        cost_estimate=pl.CostEstimate(flops=1400000000, bytes_accessed=6000000, transcendentals=600000),
    )(place, *tokens, gain, *pieces)


def norm_kernel(base, came, over, gain, first, normed):
    summed = (base[...] + came[:ROWS, :].astype(F32) + over[...].astype(F32)).astype(BF)
    first[...] = summed
    normed[...] = norm_rows(summed.astype(F32), gain[...])


def norm_call(base, came, over, gain):
    return pl.pallas_call(
        norm_kernel,
        out_shape=[jax.ShapeDtypeStruct((ROWS, 1024), BF)] * 2,
        in_specs=[VMEM] * 4,
        out_specs=[VMEM] * 2,
        cost_estimate=pl.CostEstimate(flops=2000000, bytes_accessed=2500000, transcendentals=0),
    )(base, came, over, gain)


def mlp_kernel(place, first, own, other, far, far_other, *refs):
    pieces, refs = refs[:9], refs[9:]
    base, away, over, tokens, wup, wdown, hidden, sems = refs
    pairs, lower = [], []
    for step in range(8):
        z = lax.rem(place[1] * 4 + place[4] + step, 8)
        zl = lax.rem(z, 4)
        for rx in range(4):
            ref, at = pieces[step], rx * 128
            if step == 4:
                ref, at = pieces[4 + rx // 2 * 4], rx % 2 * 128
            block = lax.div(z, 4) * 4 + lax.rem(place[0] + rx, 4)
            pairs.append((ref.at[pl.ds(at, 128), pl.ds(0, 256)],
                          wup.at[aligned(block * 128, 128, 128), aligned(zl * 256, 256, 256)]))
            lower.append((ref.at[pl.ds(at, 128), pl.ds(256, 256)], wdown.at[block * 4 + zl]))
    copies = start_copies(pairs + lower, sems)
    for i, ref in enumerate((own, other, far, far_other)):
        tokens[i * ROWS : (i + 1) * ROWS, :] = ref[...]
    for copy in copies[: len(pairs)]:
        copy.wait()
    for part in range(2):
        cols = slice(part * HALF, (part + 1) * HALF)
        inner = jnp.dot(tokens[...], wup[:, cols], preferred_element_type=F32)
        hidden[:, cols] = jax.nn.gelu(inner, approximate=True).astype(BF)
    for copy in copies[len(pairs) :]:
        copy.wait()
    for part in range(4):
        cols = slice(part * 256, part * 256 + 256)
        got = jnp.dot(hidden[...], wdown[:, part * 32 : part * 32 + 32, :].reshape(1024, 256), preferred_element_type=F32)
        base[:, cols] = first[:, cols].astype(F32) + got[:ROWS]
        away[:ROWS, cols] = got[ROWS : 2 * ROWS].astype(BF)
        over[:, cols] = got[2 * ROWS : 3 * ROWS]
        away[ROWS:, cols] = got[3 * ROWS :].astype(BF)


def mlp_call(place, first, tokens, pieces):
    return pl.pallas_call(
        mlp_kernel,
        out_shape=[wide(ROWS), wide(2 * ROWS, BF), wide(ROWS)],
        in_specs=[SMEM] + [VMEM] * 5 + [ANY] * 9,
        out_specs=[VMEM] * 3,
        scratch_shapes=[
            pltpu.VMEM((4 * ROWS, 1024), BF),
            pltpu.VMEM((1024, 1024), BF),
            pltpu.VMEM((32, 128, 256), BF),
            pltpu.VMEM((4 * ROWS, 1024), BF),
            pltpu.SemaphoreType.DMA((64,)),
        ],
        compiler_params=BIG,
        cost_estimate=pl.CostEstimate(flops=2200000000, bytes_accessed=9000000, transcendentals=600000),
    )(place, first, *tokens, *pieces)


def time_kernel(place, own, other, gain, shared, base, away, tokens, weights, packed, att, sems):
    pairs = []
    for y in range(4):
        for x in range(4):
            for rz in range(2):
                block = lax.rem(place[1] + rz, 2) * 4 + x
                pairs.append((shared.at[pl.ds(((y * 4 + x) * 2 + rz) * 128, 128)],
                              weights.at[aligned(block * 128, 128, 128), pl.ds(y * HALF, HALF)]))
    copies = start_copies(pairs, sems)
    tokens[:ROWS, :] = norm_rows(own[...].astype(F32), gain[...])
    tokens[ROWS:, :] = norm_rows(other[...].astype(F32), gain[...])
    for pair in range(4):
        for copy in copies[pair * 8 : pair * 8 + 8]:
            copy.wait()
        at = pair * 384
        packed[:, at : at + 384] = jnp.dot(
            tokens[...], weights[:, pair * HALF : pair * HALF + 384], preferred_element_type=F32).astype(BF)
        query, keys, values = (packed[:, at + i * 128 : at + i * 128 + 128] for i in range(3))
        att[:, pair * 128 : pair * 128 + 128] = attend_pair(query * 0.125, keys, values, 2)
    for pair in range(4):
        lanes = slice(pair * HALF + 384, pair * HALF + 512)
        rows = jnp.concatenate([
            jnp.concatenate([weights[block * 128 + i * 64 : block * 128 + i * 64 + 64, lanes] for block in range(8)], axis=0)
            for i in range(2)], axis=1)
        cols = slice(pair * 256, pair * 256 + 256)
        got = jnp.dot(att[...], rows, preferred_element_type=F32)
        base[:, cols] = own[:, cols].astype(F32) + got[:ROWS]
        away[:, cols] = got[ROWS:].astype(BF)


def time_call(place, own, other, gain, shared):
    return pl.pallas_call(
        time_kernel,
        out_shape=[wide(ROWS), wide(ROWS, BF)],
        in_specs=[SMEM] + [VMEM] * 3 + [ANY],
        out_specs=[VMEM] * 2,
        scratch_shapes=[
            pltpu.VMEM((2 * ROWS, 1024), BF),
            pltpu.VMEM((1024, 2048), BF),
            pltpu.VMEM((2 * ROWS, 1536), BF),
            pltpu.VMEM((2 * ROWS, 512), BF),
            pltpu.SemaphoreType.DMA((32,)),
        ],
        compiler_params=pltpu.CompilerParams(vmem_limit_bytes=24 * 1024 * 1024),
        cost_estimate=pl.CostEstimate(flops=1400000000, bytes_accessed=6000000, transcendentals=600000),
    )(place, own, other, gain, shared)


def leave_kernel(base, came, out):
    done = base[...] + came[...].astype(F32)
    left, right = done[:, :HALF].reshape(16, 8, HALF), done[:, HALF:].reshape(16, 8, HALF)
    upper = lax.broadcasted_iota(jnp.int32, (16, 8, HALF), 1) < 4
    turn = lambda v: jnp.concatenate([v[:, 4:], v[:, :4]], axis=1)
    out[:, 0] = jnp.where(upper, left, turn(right)).astype(BF)
    out[:, 1] = jnp.where(upper, turn(left), right).astype(BF)


def leave_call(base, came):
    return pl.pallas_call(
        leave_kernel,
        out_shape=jax.ShapeDtypeStruct((16, 2, 8, HALF), BF),
        in_specs=[VMEM] * 2,
        out_specs=VMEM,
        cost_estimate=pl.CostEstimate(flops=1000000, bytes_accessed=1300000, transcendentals=0),
    )(base, came).reshape(32, 8, HALF)


def arrive_kernel(came, out):
    wide_rows = came[...].astype(F32)
    for frame in range(4):
        for half in range(2):
            out[0, frame, :, half * HALF : half * HALF + HALF] = wide_rows[:, half * 4 + frame, :].astype(BF)


def arrive_call(came):
    return pl.pallas_call(
        arrive_kernel,
        out_shape=jax.ShapeDtypeStruct((1, 4, 32, 1024), BF),
        in_specs=[VMEM],
        out_specs=VMEM,
        cost_estimate=pl.CostEstimate(flops=1000000, bytes_accessed=500000, transcendentals=0),
    )(came)


def body(clip, space_gain, space_qkv, space_out, mlp_gain, mlp_up, mlp_down, time_gain, time_qkv, time_out):
    dp, fs = lax.axis_index("dp"), lax.axis_index("fsdp")
    x, zh, c, y, zl = lax.rem(fs, 4), lax.div(fs, 4), lax.rem(dp, 2), lax.rem(lax.div(dp, 2), 4), lax.div(dp, 8)
    place = jnp.stack([x, zh, y, c, zl, lax.rem(y, 2) * 2 + c]).astype(jnp.int32)
    width = clip.shape[-1]
    gains = [gain.reshape(1, width) for gain in (space_gain, mlp_gain, time_gain)]

    together = lambda *v: lax.optimization_barrier(v)
    planes = [[device(px, py, z, core) for py in range(4) for px in range(4)] for z in range(8) for core in range(2)]
    near, reach = make_shares(place, space_qkv, space_out, mlp_up, mlp_down, time_qkv, time_out)
    far = shift(reach, z=4)
    near = near, shift(near, x=-1), shift(near, x=2), shift(near, x=1)
    split = clip.reshape(4, 16, 2, width)
    keep = jnp.where(c == 0, split[:, :, 0], split[:, :, 1])
    give = jnp.where(c == 0, split[:, :, 1], split[:, :, 0])
    taken = shift(give, c=1)
    frames = jnp.where(c == 0, jnp.concatenate([keep, taken], axis=0), jnp.concatenate([taken, keep], axis=0))
    frames = lax.all_to_all(frames, "fsdp", split_axis=0, concat_axis=0, tiled=True)
    own = frames.transpose(1, 0, 2).reshape(ROWS, width)
    far, *near = together(far, *near)
    piece = far[:320]
    far = far, shift(piece, x=-1), shift(piece, x=2), shift(piece, x=1)
    mlp = stack(near)
    over = swap_chips(own)
    up, down = [mlp, shift(mlp, z=1)], [mlp, shift(mlp, z=-1)]
    over, up[1], down[1], *far = together(over, up[1], down[1], *far)
    up.append(shift(up[1], z=1))
    down.append(shift(down[1], z=-1))
    space = (*near, *far)
    shared = jnp.concatenate([reach[320:], far[0][320:]], axis=0)
    shared = lax.all_gather(shared, AXES, axis=0, tiled=True, axis_index_groups=planes)

    base, away, over = space_call(place, (own, shift(own, c=1), over, shift(over, c=1)), gains[0], space)
    away, up[2], down[2] = together(away, up[2], down[2])
    up.append(shift(up[2], z=1))
    down.append(shift(down[2], z=-1))
    came = shift(away, c=1)
    over = swap_chips((over + came[ROWS:]).astype(BF))
    over, up[3], down[3] = together(over, up[3], down[3])
    up.append(shift(up[3][:256], z=1))
    down.append(shift(down[3][256:], z=-1))
    first, normed = norm_call(base, came, over, gains[1])
    over = swap_chips(normed)
    mlp = (*down[:4], up[4], up[3], up[2], up[1], down[4])
    base, away, over = mlp_call(place, first, (normed, shift(normed, c=1), over, shift(over, c=1)), mlp)
    came = shift(away, c=1)
    over = swap_chips((over + came[ROWS:]).astype(BF))
    second = (base + came[:ROWS] + over.astype(F32)).astype(BF)

    groups = [[(2 * m + core) * 8 + k for m in range(16) for k in range(8)] for core in range(2)]
    series = lax.all_to_all(second, AXES, split_axis=0, concat_axis=0, tiled=True, axis_index_groups=groups)
    base, away = time_call(place, series, shift(series, c=1), gains[2], shared)
    done = leave_call(base, shift(away, c=1))
    return arrive_call(lax.all_to_all(done, "dp", split_axis=0, concat_axis=0, tiled=True))


def solution(mesh):
    return jax.shard_map(
        body,
        mesh=mesh,
        in_specs=(
            P(None, "dp", "fsdp", None),
            P(),
            P("fsdp", None),
            P("fsdp", None),
            P(),
            P("fsdp", None),
            P("fsdp", None),
            P(),
            P("fsdp", None),
            P("fsdp", None),
        ),
        out_specs=P(None, "dp", "fsdp", None),
        check_vma=False,
    )
```

profile of v0, /device:TPU:1, one launch (start us, length us, event | category | flops | bytes accessed | tf_op | source)
XLA Modules:
  0.0 198.0 jit_solution(13724792923327425009)
XLA Ops:
  7.1 3.3 %shard_map.100 = (bf16[448,512]{1,0:T(8,128)(2,1)}, bf16[448,512]{1,0:T(8,128)(2,1)}) custom-call(s32[6]{0:T(128)} %stack.27.place, bf16[128,3072]{1,0:T(8,128)(2,1)} %sqkv.1, bf16[128,1024]{1,0:T(8,128)(2,1)} %sproject.1, bf16[128,4096]{1,0:T(8,128)(2,1)} %up.1, bf16[512,1024]{1,0:T(8,128)(2,1)} %down.1, bf16[128,3072]{1,0:T(8,128)(2,1)} %tqkv.1, ...), custom_call_target="tpu_custom_call" | custom-call | flops 120000000 | bytes 2500000 | tf_op jit(solution)/shard_map/pallas_call | solution.py:104
  10.4 3.4 %collective-permute-start.4 = (bf16[448,512]{1,0:T(8,128)(2,1)}, bf16[448,512]{1,0:T(8,128)(2,1)S(1)}, u32[]{:S(2)}, u32[]{:S(2)}) collective-permute-start(bf16[448,512]{1,0:T(8,128)(2,1)} %get-tuple-element.37.a.refs_0_), channel_id=1, source_target_pairs={{0,3},{8,11},{64,67},{72,75},{128,131},{136,139},{192,195},{200,20... | collective-permute-start | bytes 1376264 | tf_op jit(solution)/shard_map/ppermute | solution.py:33
  14.9 6.9 %collective-permute-start.3 = (bf16[448,512]{1,0:T(8,128)(2,1)}, bf16[448,512]{1,0:T(8,128)(2,1)S(1)}, u32[]{:S(2)}, u32[]{:S(2)}) collective-permute-start(bf16[448,512]{1,0:T(8,128)(2,1)} %get-tuple-element.35), channel_id=1, source_target_pairs={{0,4},{8,12},{64,68},{72,76},{128,132},{136,140},{192,196},{200,20... | collective-permute-start | bytes 1376264 | tf_op jit(solution)/shard_map/ppermute | solution.py:33
  22.1 1.9 collective-permute-start
  24.1 0.9 collective-permute-done
  26.1 3.4 %all-to-all-start = ((bf16[8,16,1024]{2,1,0:T(8,128)(2,1)}), bf16[8,16,1024]{2,1,0:T(8,128)(2,1)S(1)}, u32[]{:S(2)}, u32[]{:S(2)}) async-start(bf16[8,16,1024]{2,1,0:T(8,128)(2,1)} %copy.20), calls=%async_computation | async-start | bytes 524288 | tf_op jit(solution)/shard_map/all_to_all | solution.py:410
  29.6 2.8 %collective-permute-done.3.refs_4_ = bf16[448,512]{1,0:T(8,128)(2,1)S(1)} collective-permute-done((bf16[448,512]{1,0:T(8,128)(2,1)}, bf16[448,512]{1,0:T(8,128)(2,1)S(1)}, u32[]{:S(2)}, u32[]{:S(2)}) %collective-permute-start.3) | collective-permute-done | bytes 458784 | tf_op jit(solution)/shard_map/ppermute | solution.py:33
  32.4 5.7 %collective-permute-done.6.d.refs_3_ = bf16[448,512]{1,0:T(8,128)(2,1)S(1)} collective-permute-done((bf16[448,512]{1,0:T(8,128)(2,1)}, bf16[448,512]{1,0:T(8,128)(2,1)S(1)}, u32[]{:S(2)}, u32[]{:S(2)}) %collective-permute-start.6) | collective-permute-done | bytes 458784 | tf_op jit(solution)/shard_map/ppermute | solution.py:33
  39.0 2.0 shard_map.101.refs_0_
  40.9 7.9 %collective-permute-start.7 = (bf16[512,512]{1,0:T(8,128)(2,1)}, bf16[512,512]{1,0:T(8,128)(2,1)S(1)}, u32[]{:S(2)}, u32[]{:S(2)}) collective-permute-start(bf16[512,512]{1,0:T(8,128)(2,1)} %shard_map.101.refs_0_), channel_id=1, source_target_pairs={{0,64},{8,72},{64,128},{72,136},{128,192},{136,200},{192,4},{200,1... | collective-permute-start | bytes 1572872 | tf_op jit(solution)/shard_map/ppermute | solution.py:33
  48.9 2.7 %collective-permute-start.9 = (bf16[320,512]{1,0:T(8,128)(2,1)S(1)}, bf16[320,512]{1,0:T(8,128)(2,1)S(1)}, u32[]{:S(2)}, u32[]{:S(2)}) collective-permute-start(bf16[320,512]{1,0:T(8,128)(2,1)S(1)} %slice.34), channel_id=1, source_target_pairs={{0,3},{8,11},{64,67},{72,75},{128,131},{136,139},{192,195},{200,20... | collective-permute-start | bytes 983048 | tf_op jit(solution)/shard_map/ppermute | solution.py:33
  51.7 1.4 collective-permute-start.2
  53.1 0.9 slice.40
  54.0 2.3 %collective-permute-done.11.refs_7_ = bf16[320,512]{1,0:T(8,128)(2,1)S(1)} collective-permute-done((bf16[320,512]{1,0:T(8,128)(2,1)S(1)}, bf16[320,512]{1,0:T(8,128)(2,1)S(1)}, u32[]{:S(2)}, u32[]{:S(2)}) %collective-permute-start.11) | collective-permute-done | bytes 327712 | tf_op jit(solution)/shard_map/ppermute | solution.py:33
  56.3 1.0 collective-permute-done.2.far
  57.3 2.0 %collective-permute-done.8.refs_1_ = bf16[512,512]{1,0:T(8,128)(2,1)S(1)} collective-permute-done((bf16[512,512]{1,0:T(8,128)(2,1)}, bf16[512,512]{1,0:T(8,128)(2,1)S(1)}, u32[]{:S(2)}, u32[]{:S(2)}) %collective-permute-start.8) | collective-permute-done | bytes 524320 | tf_op jit(solution)/shard_map/ppermute | solution.py:33
  60.1 2.6 %collective-permute-start.13 = (bf16[512,512]{1,0:T(8,128)(2,1)S(1)}, bf16[512,512]{1,0:T(8,128)(2,1)S(1)}, u32[]{:S(2)}, u32[]{:S(2)}) collective-permute-start(bf16[512,512]{1,0:T(8,128)(2,1)S(1)} %collective-permute-done.7.refs_7_), channel_id=1, source_target_pairs={{0,64},{8,72},{64,128},{72,136},{128,192},{136,200},{192,4},{200,1... | collective-permute-start | bytes 1572872 | tf_op jit(solution)/shard_map/ppermute | solution.py:33
  62.7 1.2 collective-permute-start.14
  63.9 4.1 %collective-permute-start.1 = (bf16[128,1024]{1,0:T(8,128)(2,1)S(1)}, bf16[128,1024]{1,0:T(8,128)(2,1)S(1)}, u32[]{:S(2)}, u32[]{:S(2)}) collective-permute-start(bf16[128,1024]{1,0:T(8,128)(2,1)S(1)} %bitcast.44), channel_id=1, source_target_pairs={{0,8},{8,0},{64,72},{72,64},{128,136},{136,128},{192,200},{200,192... | collective-permute-start | bytes 786440 | tf_op jit(solution)/shard_map/ppermute | solution.py:33
  68.0 1.2 collective-permute-done.1.other
  70.3 6.9 %shard_map.102 = (f32[128,1024]{1,0:T(8,128)}, bf16[256,1024]{1,0:T(8,128)(2,1)}, f32[128,1024]{1,0:T(8,128)}) custom-call(s32[6]{0:T(128)} %stack.27.place, bf16[128,1024]{1,0:T(8,128)(2,1)} %bitcast.45, bf16[128,1024]{1,0:T(8,128)(2,1)} %copy-done.27, bf16[128,1024]{1,0:T(8,128)(2,1)} %copy-done.21, bf16[128,1024]{1,0:T(8,128)(2,1)} %copy-done.28, ...), custom_call_target="tpu_custom_call" | custom-call | flops 1400000000 | bytes 6000000 | tf_op jit(solution)/shard_map/pallas_call | solution.py:222
  77.2 1.2 collective-permute-start.15
  78.4 1.5 collective-permute-start.17
  79.9 1.7 collective-permute-start.18
  81.6 1.3 add_convert_fusion.2
  82.8 1.4 collective-permute-start.16
  84.2 9.5 %collective-permute-done.17.refs_5_ = bf16[512,512]{1,0:T(8,128)(2,1)S(1)} collective-permute-done((bf16[512,512]{1,0:T(8,128)(2,1)S(1)}, bf16[512,512]{1,0:T(8,128)(2,1)S(1)}, u32[]{:S(2)}, u32[]{:S(2)}) %collective-permute-start.17) | collective-permute-done | bytes 524320 | tf_op jit(solution)/shard_map/ppermute | solution.py:33
  94.6 2.3 %shard_map.103 = (bf16[128,1024]{1,0:T(8,128)(2,1)}, bf16[128,1024]{1,0:T(8,128)(2,1)}) custom-call(f32[128,1024]{1,0:T(8,128)} %get-tuple-element.47.base, bf16[256,1024]{1,0:T(8,128)(2,1)} %copy-done.4, bf16[128,1024]{1,0:T(8,128)(2,1)} %copy-done.9, f32[1,1024]{1,0:T(1,128)} %bitcast.46), custom_call_target="tpu_custom_call" | custom-call | flops 2000000 | bytes 2500000 | tf_op jit(solution)/shard_map/pallas_call | solution.py:247
  96.8 1.3 collective-permute-start.20
  98.1 1.0 collective-permute-start.19
  99.4 2.6 %collective-permute-start.23 = (bf16[256,512]{1,0:T(8,128)(2,1)S(1)}, bf16[256,512]{1,0:T(8,128)(2,1)S(1)}, u32[]{:S(2)}, u32[]{:S(2)}) collective-permute-start(bf16[256,512]{1,0:T(8,128)(2,1)S(1)} %slice.37), channel_id=1, source_target_pairs={{0,196},{8,204},{64,0},{72,8},{128,64},{136,72},{192,128},{200,136... | collective-permute-start | bytes 786440 | tf_op jit(solution)/shard_map/ppermute | solution.py:33
  102.0 2.3 %collective-permute-done.20.far = bf16[128,1024]{1,0:T(8,128)(2,1)S(1)} collective-permute-done((bf16[128,1024]{1,0:T(8,128)(2,1)}, bf16[128,1024]{1,0:T(8,128)(2,1)S(1)}, u32[]{:S(2)}, u32[]{:S(2)}) %collective-permute-start.20) | collective-permute-done | bytes 262176 | tf_op jit(solution)/shard_map/ppermute | solution.py:37
  104.3 1.6 collective-permute-start.21
  105.8 2.6 %collective-permute-done.22.refs_4_ = bf16[256,512]{1,0:T(8,128)(2,1)S(1)} collective-permute-done((bf16[256,512]{1,0:T(8,128)(2,1)S(1)}, bf16[256,512]{1,0:T(8,128)(2,1)S(1)}, u32[]{:S(2)}, u32[]{:S(2)}) %collective-permute-start.22) | collective-permute-done | bytes 262176 | tf_op jit(solution)/shard_map/ppermute | solution.py:33
  109.4 7.5 %shard_map.104 = (f32[128,1024]{1,0:T(8,128)}, bf16[256,1024]{1,0:T(8,128)(2,1)}, f32[128,1024]{1,0:T(8,128)}) custom-call(s32[6]{0:T(128)} %stack.27.place, bf16[128,1024]{1,0:T(8,128)(2,1)} %get-tuple-element.56.first, bf16[128,1024]{1,0:T(8,128)(2,1)} %get-tuple-element.57.own, bf16[128,1024]{1,0:T(8,128)(2,1)} %copy-done.23, ...), custom_call_target="tpu_custom_call" | custom-call | flops 2200000000 | bytes 9000000 | tf_op jit(solution)/shard_map/pallas_call | solution.py:292
  117.7 1.7 collective-permute-done.24
  119.4 1.1 add_convert_fusion.1
  120.7 7.4 %collective-permute-done.25 = bf16[128,1024]{1,0:T(8,128)(2,1)S(1)} collective-permute-done((bf16[128,1024]{1,0:T(8,128)(2,1)S(1)}, bf16[128,1024]{1,0:T(8,128)(2,1)S(1)}, u32[]{:S(2)}, u32[]{:S(2)}) %collective-permute-start.25) | collective-permute-done | bytes 262176 | tf_op jit(solution)/shard_map/ppermute | solution.py:37
  128.2 1.1 fusion
  130.8 25.2 %all_to_all.21 = bf16[128,2,512]{2,1,0:T(2,128)(2,1)S(1)} all-to-all(bf16[128,2,512]{2,1,0:T(2,128)(2,1)S(1)} %reshape.30), channel_id=1, replica_groups={{0,1,2,3,4,5,6,7,16,17,18,19,20,21,22,23,32,33,34,35,36,37,38,39,48,49,..., dimensions={0} | all-to-all | bytes 524288 | tf_op jit(solution)/shard_map/all_to_all | solution.py:443
  156.4 3.0 %collective-permute-start.26 = (bf16[128,1024]{1,0:T(8,128)(2,1)S(1)}, bf16[128,1024]{1,0:T(8,128)(2,1)S(1)}, u32[]{:S(2)}, u32[]{:S(2)}) collective-permute-start(bf16[128,1024]{1,0:T(8,128)(2,1)S(1)} %bitcast.36), channel_id=1, source_target_pairs={{0,8},{8,0},{64,72},{72,64},{128,136},{136,128},{192,200},{200,192... | collective-permute-start | bytes 786440 | tf_op jit(solution)/shard_map/ppermute | solution.py:33
  159.4 1.2 collective-permute-done.26.other
  160.6 2.2 %copy-done.2 = bf16[4096,512]{1,0:T(8,128)(2,1)S(1)} copy-done((bf16[4096,512]{1,0:T(8,128)(2,1)S(1)}, bf16[4096,512]{1,0:T(8,128)(2,1)}, u32[]{:S(2)}) %copy-start.2) | copy-done | bytes 4194328
  162.8 5.7 %shard_map.105 = (f32[128,1024]{1,0:T(8,128)S(1)}, bf16[128,1024]{1,0:T(8,128)(2,1)S(1)}) custom-call(s32[6]{0:T(128)S(1)} %copy-done.1, bf16[128,1024]{1,0:T(8,128)(2,1)S(1)} %bitcast.37, bf16[128,1024]{1,0:T(8,128)(2,1)S(1)} %collective-permute-done.26.other, f32[1,1024]{1,0:T(1,128)S(1)} %bitcast.38, bf16[4096,512]{1,0:T(8,128)(2,1)S(1)} %copy-done.2), custom_call_target="tpu_custom_call" | custom-call | flops 1400000000 | bytes 6000000 | tf_op jit(solution)/shard_map/pallas_call | solution.py:340
  169.7 1.2 collective-permute-done.27.came
  171.5 1.9 shard_map.106
  173.4 15.8 %all_to_all.22.came = bf16[32,8,512]{2,1,0:T(8,128)(2,1)} all-to-all(bf16[32,8,512]{2,1,0:T(8,128)(2,1)} %bitcast.42), channel_id=1, replica_groups=mesh['dp'=32,'fsdp'=8] {'dp'}, dimensions={0} | all-to-all | bytes 524288 | tf_op jit(solution)/shard_map/all_to_all | solution.py:446
  189.2 1.9 shard_map.107
  (102 shorter events, 12.6 us)
Async XLA Ops:
  6.5 15.3 %copy-start.10 = (bf16[1,4,32,1024]{3,2,1,0:T(8,128)(2,1)S(1)}, bf16[1,4,32,1024]{3,2,1,0:T(8,128)(2,1)}, u32[]{:S(2)}) copy-start(bf16[1,4,32,1024]{3,2,1,0:T(8,128)(2,1)} %param.10) | copy-start | bytes 786436
  10.4 22.0 %collective-permute-start.4 = (bf16[448,512]{1,0:T(8,128)(2,1)}, bf16[448,512]{1,0:T(8,128)(2,1)S(1)}, u32[]{:S(2)}, u32[]{:S(2)}) collective-permute-start(bf16[448,512]{1,0:T(8,128)(2,1)} %get-tuple-element.37.a.refs_0_), channel_id=1, source_target_pairs={{0,3},{8,11},{64,67},{72,75},{128,131},{136,139},{192,195},{200,20... | collective-permute-start | bytes 1376264 | tf_op jit(solution)/shard_map/ppermute | solution.py:33
  13.8 18.6 %collective-permute-start.5 = (bf16[448,512]{1,0:T(8,128)(2,1)}, bf16[448,512]{1,0:T(8,128)(2,1)S(1)}, u32[]{:S(2)}, u32[]{:S(2)}) collective-permute-start(bf16[448,512]{1,0:T(8,128)(2,1)} %get-tuple-element.37.a.refs_0_), channel_id=1, source_target_pairs={{0,2},{8,10},{64,66},{72,74},{128,130},{136,138},{192,194},{200,20... | collective-permute-start | bytes 1376264 | tf_op jit(solution)/shard_map/ppermute | solution.py:33
  14.3 23.8 %collective-permute-start.6 = (bf16[448,512]{1,0:T(8,128)(2,1)}, bf16[448,512]{1,0:T(8,128)(2,1)S(1)}, u32[]{:S(2)}, u32[]{:S(2)}) collective-permute-start(bf16[448,512]{1,0:T(8,128)(2,1)} %get-tuple-element.37.a.refs_0_), channel_id=1, source_target_pairs={{0,1},{8,9},{64,65},{72,73},{128,129},{136,137},{192,193},{200,201... | collective-permute-start | bytes 1376264 | tf_op jit(solution)/shard_map/ppermute | solution.py:33
  14.9 17.5 %collective-permute-start.3 = (bf16[448,512]{1,0:T(8,128)(2,1)}, bf16[448,512]{1,0:T(8,128)(2,1)S(1)}, u32[]{:S(2)}, u32[]{:S(2)}) collective-permute-start(bf16[448,512]{1,0:T(8,128)(2,1)} %get-tuple-element.35), channel_id=1, source_target_pairs={{0,4},{8,12},{64,68},{72,76},{128,132},{136,140},{192,196},{200,20... | collective-permute-start | bytes 1376264 | tf_op jit(solution)/shard_map/ppermute | solution.py:33
  22.1 2.9 %collective-permute-start = (bf16[4,16,1024]{2,0,1:T(4,128)(2,1)S(1)}, bf16[4,16,1024]{2,0,1:T(4,128)(2,1)S(1)}, u32[]{:S(2)}, u32[]{:S(2)}) collective-permute-start(bf16[4,16,1024]{2,0,1:T(4,128)(2,1)S(1)} %fusion.1), channel_id=1, source_target_pairs={{0,8},{8,0},{64,72},{72,64},{128,136},{136,128},{192,200},{200,192... | collective-permute-start | bytes 393224 | tf_op jit(solution)/shard_map/ppermute | solution.py:33
  26.1 25.5 %all-to-all-start = ((bf16[8,16,1024]{2,1,0:T(8,128)(2,1)}), bf16[8,16,1024]{2,1,0:T(8,128)(2,1)S(1)}, u32[]{:S(2)}, u32[]{:S(2)}) async-start(bf16[8,16,1024]{2,1,0:T(8,128)(2,1)} %copy.20), calls=%async_computation | async-start | bytes 524288 | tf_op jit(solution)/shard_map/all_to_all | solution.py:410
  29.5 131.1 %all-gather.2.cloned.1.call-start = ((), (), s32[]{:S(2)}) async-start(), calls=%async_computation.3 | async-start | bytes 4456448 | tf_op jit(solution)/shard_map/all_gather | solution.py:423
  32.4 37.2 %copy-start.8 = (bf16[448,512]{1,0:T(8,128)(2,1)}, bf16[448,512]{1,0:T(8,128)(2,1)S(1)}, u32[]{:S(2)}) copy-start(bf16[448,512]{1,0:T(8,128)(2,1)S(1)} %collective-permute-done.3.refs_4_) | copy-start | bytes 1376260
  32.4 6.4 %copy-start.5 = (bf16[448,512]{1,0:T(8,128)(2,1)}, bf16[448,512]{1,0:T(8,128)(2,1)S(1)}, u32[]{:S(2)}) copy-start(bf16[448,512]{1,0:T(8,128)(2,1)S(1)} %collective-permute-done.4.b.refs_1_) | copy-start | bytes 1376260
  32.4 6.4 %copy-start.6 = (bf16[448,512]{1,0:T(8,128)(2,1)}, bf16[448,512]{1,0:T(8,128)(2,1)S(1)}, u32[]{:S(2)}) copy-start(bf16[448,512]{1,0:T(8,128)(2,1)S(1)} %collective-permute-done.5.c.refs_2_) | copy-start | bytes 1376260
  38.2 13.5 %collective-permute-start.10 = (bf16[320,512]{1,0:T(8,128)(2,1)S(1)}, bf16[320,512]{1,0:T(8,128)(2,1)}, u32[]{:S(2)}, u32[]{:S(2)}) collective-permute-start(bf16[320,512]{1,0:T(8,128)(2,1)S(1)} %slice.34), channel_id=1, source_target_pairs={{0,2},{8,10},{64,66},{72,74},{128,130},{136,138},{192,194},{200,20... | collective-permute-start | bytes 983048 | tf_op jit(solution)/shard_map/ppermute | solution.py:33
  40.9 16.4 %collective-permute-start.7 = (bf16[512,512]{1,0:T(8,128)(2,1)}, bf16[512,512]{1,0:T(8,128)(2,1)S(1)}, u32[]{:S(2)}, u32[]{:S(2)}) collective-permute-start(bf16[512,512]{1,0:T(8,128)(2,1)} %shard_map.101.refs_0_), channel_id=1, source_target_pairs={{0,64},{8,72},{64,128},{72,136},{128,192},{136,200},{192,4},{200,1... | collective-permute-start | bytes 1572872 | tf_op jit(solution)/shard_map/ppermute | solution.py:33
  48.9 10.5 %collective-permute-start.8 = (bf16[512,512]{1,0:T(8,128)(2,1)}, bf16[512,512]{1,0:T(8,128)(2,1)S(1)}, u32[]{:S(2)}, u32[]{:S(2)}) collective-permute-start(bf16[512,512]{1,0:T(8,128)(2,1)} %shard_map.101.refs_0_), channel_id=1, source_target_pairs={{0,196},{8,204},{64,0},{72,8},{128,64},{136,72},{192,128},{200,136... | collective-permute-start | bytes 1572872 | tf_op jit(solution)/shard_map/ppermute | solution.py:33
  48.9 7.4 %collective-permute-start.11 = (bf16[320,512]{1,0:T(8,128)(2,1)S(1)}, bf16[320,512]{1,0:T(8,128)(2,1)S(1)}, u32[]{:S(2)}, u32[]{:S(2)}) collective-permute-start(bf16[320,512]{1,0:T(8,128)(2,1)S(1)} %slice.34), channel_id=1, source_target_pairs={{0,1},{8,9},{64,65},{72,73},{128,129},{136,137},{192,193},{200,201... | collective-permute-start | bytes 983048 | tf_op jit(solution)/shard_map/ppermute | solution.py:33
  48.9 7.4 %collective-permute-start.9 = (bf16[320,512]{1,0:T(8,128)(2,1)S(1)}, bf16[320,512]{1,0:T(8,128)(2,1)S(1)}, u32[]{:S(2)}, u32[]{:S(2)}) collective-permute-start(bf16[320,512]{1,0:T(8,128)(2,1)S(1)} %slice.34), channel_id=1, source_target_pairs={{0,3},{8,11},{64,67},{72,75},{128,131},{136,139},{192,195},{200,20... | collective-permute-start | bytes 983048 | tf_op jit(solution)/shard_map/ppermute | solution.py:33
  51.7 17.9 %copy-start.11 = (bf16[16,8,1024]{2,1,0:T(8,128)(2,1)}, bf16[16,8,1024]{2,1,0:T(8,128)(2,1)S(1)}, u32[]{:S(2)}) copy-start(bf16[16,8,1024]{2,1,0:T(8,128)(2,1)S(1)} %copy.28) | copy-start | bytes 786436
  51.7 5.6 %collective-permute-start.2 = (bf16[128,1024]{1,0:T(8,128)(2,1)S(1)}, bf16[128,1024]{1,0:T(8,128)(2,1)S(1)}, u32[]{:S(2)}, u32[]{:S(2)}) collective-permute-start(bf16[128,1024]{1,0:T(8,128)(2,1)S(1)} %bitcast.43), channel_id=1, source_target_pairs={{0,16},{8,24},{64,80},{72,88},{128,144},{136,152},{192,208},{200,2... | collective-permute-start | bytes 786440 | tf_op jit(solution)/shard_map/ppermute | solution.py:37
  56.3 13.3 %copy-start.19 = (bf16[320,512]{1,0:T(8,128)(2,1)}, bf16[320,512]{1,0:T(8,128)(2,1)S(1)}, u32[]{:S(2)}) copy-start(bf16[320,512]{1,0:T(8,128)(2,1)S(1)} %collective-permute-done.11.refs_7_) | copy-start | bytes 983044
  56.3 13.3 %copy-start.20 = (bf16[320,512]{1,0:T(8,128)(2,1)}, bf16[320,512]{1,0:T(8,128)(2,1)S(1)}, u32[]{:S(2)}) copy-start(bf16[320,512]{1,0:T(8,128)(2,1)S(1)} %collective-permute-done.9.refs_5_) | copy-start | bytes 983044
  57.3 12.3 %copy-start.21 = (bf16[128,1024]{1,0:T(8,128)(2,1)}, bf16[128,1024]{1,0:T(8,128)(2,1)S(1)}, u32[]{:S(2)}) copy-start(bf16[128,1024]{1,0:T(8,128)(2,1)S(1)} %collective-permute-done.2.far) | copy-start | bytes 786436
  57.3 39.5 %copy-start.15 = (bf16[512,512]{1,0:T(8,128)(2,1)}, bf16[512,512]{1,0:T(8,128)(2,1)S(1)}, u32[]{:S(2)}) copy-start(bf16[512,512]{1,0:T(8,128)(2,1)S(1)} %collective-permute-done.7.refs_7_) | copy-start | bytes 1572868
  59.3 37.5 %copy-start.16 = (bf16[512,512]{1,0:T(8,128)(2,1)}, bf16[512,512]{1,0:T(8,128)(2,1)S(1)}, u32[]{:S(2)}) copy-start(bf16[512,512]{1,0:T(8,128)(2,1)S(1)} %collective-permute-done.8.refs_1_) | copy-start | bytes 1572868
  60.1 17.0 %collective-permute-start.13 = (bf16[512,512]{1,0:T(8,128)(2,1)S(1)}, bf16[512,512]{1,0:T(8,128)(2,1)S(1)}, u32[]{:S(2)}, u32[]{:S(2)}) collective-permute-start(bf16[512,512]{1,0:T(8,128)(2,1)S(1)} %collective-permute-done.7.refs_7_), channel_id=1, source_target_pairs={{0,64},{8,72},{64,128},{72,136},{128,192},{136,200},{192,4},{200,1... | collective-permute-start | bytes 1572872 | tf_op jit(solution)/shard_map/ppermute | solution.py:33
  62.7 14.5 %collective-permute-start.14 = (bf16[512,512]{1,0:T(8,128)(2,1)S(1)}, bf16[512,512]{1,0:T(8,128)(2,1)S(1)}, u32[]{:S(2)}, u32[]{:S(2)}) collective-permute-start(bf16[512,512]{1,0:T(8,128)(2,1)S(1)} %collective-permute-done.8.refs_1_), channel_id=1, source_target_pairs={{0,196},{8,204},{64,0},{72,8},{128,64},{136,72},{192,128},{200,136... | collective-permute-start | bytes 1572872 | tf_op jit(solution)/shard_map/ppermute | solution.py:33
  63.9 5.3 %collective-permute-start.1 = (bf16[128,1024]{1,0:T(8,128)(2,1)S(1)}, bf16[128,1024]{1,0:T(8,128)(2,1)S(1)}, u32[]{:S(2)}, u32[]{:S(2)}) collective-permute-start(bf16[128,1024]{1,0:T(8,128)(2,1)S(1)} %bitcast.44), channel_id=1, source_target_pairs={{0,8},{8,0},{64,72},{72,64},{128,136},{136,128},{192,200},{200,192... | collective-permute-start | bytes 786440 | tf_op jit(solution)/shard_map/ppermute | solution.py:33
  68.0 1.5 collective-permute-start.12
  77.2 16.6 %copy-start.17 = (bf16[512,512]{1,0:T(8,128)(2,1)}, bf16[512,512]{1,0:T(8,128)(2,1)S(1)}, u32[]{:S(2)}) copy-start(bf16[512,512]{1,0:T(8,128)(2,1)S(1)} %collective-permute-done.13.refs_6_) | copy-start | bytes 1572868
  77.2 16.6 %copy-start.18 = (bf16[512,512]{1,0:T(8,128)(2,1)}, bf16[512,512]{1,0:T(8,128)(2,1)S(1)}, u32[]{:S(2)}) copy-start(bf16[512,512]{1,0:T(8,128)(2,1)S(1)} %collective-permute-done.14.refs_2_) | copy-start | bytes 1572868
  77.2 4.4 %collective-permute-start.15 = (bf16[256,1024]{1,0:T(8,128)(2,1)}, bf16[256,1024]{1,0:T(8,128)(2,1)S(1)}, u32[]{:S(2)}, u32[]{:S(2)}) collective-permute-start(bf16[256,1024]{1,0:T(8,128)(2,1)} %get-tuple-element.51), channel_id=1, source_target_pairs={{0,8},{8,0},{64,72},{72,64},{128,136},{136,128},{192,200},{200,192... | collective-permute-start | bytes 1572872 | tf_op jit(solution)/shard_map/ppermute | solution.py:33
  78.4 15.4 %collective-permute-start.17 = (bf16[512,512]{1,0:T(8,128)(2,1)S(1)}, bf16[512,512]{1,0:T(8,128)(2,1)S(1)}, u32[]{:S(2)}, u32[]{:S(2)}) collective-permute-start(bf16[512,512]{1,0:T(8,128)(2,1)S(1)} %collective-permute-done.13.refs_6_), channel_id=1, source_target_pairs={{0,64},{8,72},{64,128},{72,136},{128,192},{136,200},{192,4},{200,1... | collective-permute-start | bytes 1572872 | tf_op jit(solution)/shard_map/ppermute | solution.py:33
  79.9 13.9 %collective-permute-start.18 = (bf16[512,512]{1,0:T(8,128)(2,1)S(1)}, bf16[512,512]{1,0:T(8,128)(2,1)S(1)}, u32[]{:S(2)}, u32[]{:S(2)}) collective-permute-start(bf16[512,512]{1,0:T(8,128)(2,1)S(1)} %collective-permute-done.14.refs_2_), channel_id=1, source_target_pairs={{0,196},{8,204},{64,0},{72,8},{128,64},{136,72},{192,128},{200,136... | collective-permute-start | bytes 1572872 | tf_op jit(solution)/shard_map/ppermute | solution.py:33
  81.6 12.3 %copy-start.4 = (bf16[256,1024]{1,0:T(8,128)(2,1)}, bf16[256,1024]{1,0:T(8,128)(2,1)S(1)}, u32[]{:S(2)}) copy-start(bf16[256,1024]{1,0:T(8,128)(2,1)S(1)} %collective-permute-done.15.came) | copy-start | bytes 1572868
  82.8 10.9 %collective-permute-start.16 = (bf16[128,1024]{1,0:T(8,128)(2,1)S(1)}, bf16[128,1024]{1,0:T(8,128)(2,1)S(1)}, u32[]{:S(2)}, u32[]{:S(2)}) collective-permute-start(bf16[128,1024]{1,0:T(8,128)(2,1)S(1)} %add_convert_fusion.2), channel_id=1, source_target_pairs={{0,16},{8,24},{64,80},{72,88},{128,144},{136,152},{192,208},{200,2... | collective-permute-start | bytes 786440 | tf_op jit(solution)/shard_map/ppermute | solution.py:37
  93.8 14.7 %copy-start.13 = (bf16[512,512]{1,0:T(8,128)(2,1)}, bf16[512,512]{1,0:T(8,128)(2,1)S(1)}, u32[]{:S(2)}) copy-start(bf16[512,512]{1,0:T(8,128)(2,1)S(1)} %collective-permute-done.17.refs_5_) | copy-start | bytes 1572868
  93.8 14.7 %copy-start.14 = (bf16[512,512]{1,0:T(8,128)(2,1)}, bf16[512,512]{1,0:T(8,128)(2,1)S(1)}, u32[]{:S(2)}) copy-start(bf16[512,512]{1,0:T(8,128)(2,1)S(1)} %collective-permute-done.18.refs_3_) | copy-start | bytes 1572868
  96.8 7.4 %collective-permute-start.20 = (bf16[128,1024]{1,0:T(8,128)(2,1)}, bf16[128,1024]{1,0:T(8,128)(2,1)S(1)}, u32[]{:S(2)}, u32[]{:S(2)}) collective-permute-start(bf16[128,1024]{1,0:T(8,128)(2,1)} %get-tuple-element.57.own), channel_id=1, source_target_pairs={{0,16},{8,24},{64,80},{72,88},{128,144},{136,152},{192,208},{200,2... | collective-permute-start | bytes 786440 | tf_op jit(solution)/shard_map/ppermute | solution.py:37
  98.1 7.7 %collective-permute-start.19 = (bf16[128,1024]{1,0:T(8,128)(2,1)}, bf16[128,1024]{1,0:T(8,128)(2,1)S(1)}, u32[]{:S(2)}, u32[]{:S(2)}) collective-permute-start(bf16[128,1024]{1,0:T(8,128)(2,1)} %get-tuple-element.57.own), channel_id=1, source_target_pairs={{0,8},{8,0},{64,72},{72,64},{128,136},{136,128},{192,200},{200,192... | collective-permute-start | bytes 786440 | tf_op jit(solution)/shard_map/ppermute | solution.py:33
  99.1 9.3 %collective-permute-start.22 = (bf16[256,512]{1,0:T(8,128)(2,1)S(1)}, bf16[256,512]{1,0:T(8,128)(2,1)S(1)}, u32[]{:S(2)}, u32[]{:S(2)}) collective-permute-start(bf16[256,512]{1,0:T(8,128)(2,1)S(1)} %slice.36), channel_id=1, source_target_pairs={{0,64},{8,72},{64,128},{72,136},{128,192},{136,200},{192,4},{200,1... | collective-permute-start | bytes 786440 | tf_op jit(solution)/shard_map/ppermute | solution.py:33
  99.4 9.0 %collective-permute-start.23 = (bf16[256,512]{1,0:T(8,128)(2,1)S(1)}, bf16[256,512]{1,0:T(8,128)(2,1)S(1)}, u32[]{:S(2)}, u32[]{:S(2)}) collective-permute-start(bf16[256,512]{1,0:T(8,128)(2,1)S(1)} %slice.37), channel_id=1, source_target_pairs={{0,196},{8,204},{64,0},{72,8},{128,64},{136,72},{192,128},{200,136... | collective-permute-start | bytes 786440 | tf_op jit(solution)/shard_map/ppermute | solution.py:33
  104.3 4.3 %copy-start.22 = (bf16[128,1024]{1,0:T(8,128)(2,1)}, bf16[128,1024]{1,0:T(8,128)(2,1)S(1)}, u32[]{:S(2)}) copy-start(bf16[128,1024]{1,0:T(8,128)(2,1)S(1)} %collective-permute-done.20.far) | copy-start | bytes 786436
  104.3 4.2 %collective-permute-start.21 = (bf16[128,1024]{1,0:T(8,128)(2,1)S(1)}, bf16[128,1024]{1,0:T(8,128)(2,1)S(1)}, u32[]{:S(2)}, u32[]{:S(2)}) collective-permute-start(bf16[128,1024]{1,0:T(8,128)(2,1)S(1)} %collective-permute-done.20.far), channel_id=1, source_target_pairs={{0,8},{8,0},{64,72},{72,64},{128,136},{136,128},{192,200},{200,192... | collective-permute-start | bytes 786440 | tf_op jit(solution)/shard_map/ppermute | solution.py:33
  116.8 43.7 %copy-start.1 = (s32[6]{0:T(128)S(1)}, s32[6]{0:T(128)}, u32[]{:S(2)}) copy-start(s32[6]{0:T(128)} %stack.27.place) | copy-start | bytes 76
  116.8 43.7 %copy-start.3 = (f32[1024]{0:T(1024)S(1)}, f32[1024]{0:T(1024)}, u32[]{:S(2)}) copy-start(f32[1024]{0:T(1024)} %param.17) | copy-start | bytes 12292
  116.9 2.6 %collective-permute-start.24 = (bf16[256,1024]{1,0:T(8,128)(2,1)}, bf16[256,1024]{1,0:T(8,128)(2,1)S(1)}, u32[]{:S(2)}, u32[]{:S(2)}) collective-permute-start(bf16[256,1024]{1,0:T(8,128)(2,1)} %get-tuple-element.61), channel_id=1, source_target_pairs={{0,8},{8,0},{64,72},{72,64},{128,136},{136,128},{192,200},{200,192... | collective-permute-start | bytes 1572872 | tf_op jit(solution)/shard_map/ppermute | solution.py:33
  120.5 7.6 %collective-permute-start.25 = (bf16[128,1024]{1,0:T(8,128)(2,1)S(1)}, bf16[128,1024]{1,0:T(8,128)(2,1)S(1)}, u32[]{:S(2)}, u32[]{:S(2)}) collective-permute-start(bf16[128,1024]{1,0:T(8,128)(2,1)S(1)} %add_convert_fusion.1), channel_id=1, source_target_pairs={{0,16},{8,24},{64,80},{72,88},{128,144},{136,152},{192,208},{200,2... | collective-permute-start | bytes 786440 | tf_op jit(solution)/shard_map/ppermute | solution.py:37
  156.4 4.2 %collective-permute-start.26 = (bf16[128,1024]{1,0:T(8,128)(2,1)S(1)}, bf16[128,1024]{1,0:T(8,128)(2,1)S(1)}, u32[]{:S(2)}, u32[]{:S(2)}) collective-permute-start(bf16[128,1024]{1,0:T(8,128)(2,1)S(1)} %bitcast.36), channel_id=1, source_target_pairs={{0,8},{8,0},{64,72},{72,64},{128,136},{136,128},{192,200},{200,192... | collective-permute-start | bytes 786440 | tf_op jit(solution)/shard_map/ppermute | solution.py:33
  169.3 1.5 collective-permute-start.27
  (11 other events, 11.8 us)
Sparse Core Ops, SparseCore 0:
  60.3 64.1 all-gather.1
where the time goes:
time: 199 us; the launch traced here: 198 us
  starting transfers between devices  54.1 us (27%)
  waiting for transfers between devices  42.3 us (21%)
  blocking collectives  41 us (21%)
  Pallas kernels  31.4 us (16%)
  between operations  13.8 us (7%)
  local copies, waits for them, and re-layouts  9.98 us (5%)
  other arithmetic  5.48 us (3%)
    ppermute x24, starting transfers between devices, shift(): return lax.ppermute(v, AXES, pairs)  46.4 us
    ppermute x24, waiting for transfers between devices, shift(): return lax.ppermute(v, AXES, pairs)  31.5 us
    all_to_all x1, blocking collectives, body(): lax.all_to_all(second, AXES, split_axis=0, concat_axis=0, tiled=True, axi...  25.2 us
    all_to_all x1, blocking collectives, body(): lax.all_to_all(done, 'dp', split_axis=0, concat_axis=0, tiled=True)  15.8 us
    ppermute x4, waiting for transfers between devices, swap_chips(): lax.ppermute(v, AXES, [(device(a, b, d, e), device(a, b ^ 1, d, e)) for a...  10.7 us
    pallas_call x1, Pallas kernels, mlp_call(): pl.pallas_call(mlp_kernel, out_shape=[wide(ROWS), wide(2 * ROWS, BF), wid...  7.46 us
    unnamed x62, local copies, waits for them, and re-layouts  6.89 us
    pallas_call x1, Pallas kernels, space_call(): pl.pallas_call(space_kernel, out_shape=[wide(ROWS), wide(2 * ROWS, BF), w...  6.87 us
  transfers between devices with their start and end apart: 30, of which 15 were waited for; matrix products, arithmetic and copies ran while one was open for 4% of the time, Pallas kernels for 9%

commit v1 on v0

--- a/solution.py
+++ b/solution.py
@@ -61,7 +61,11 @@
                   sheads, srows, ups, downs, theads, trows, sems):
     y, c, zl, quarter = place[2], place[3], place[4], place[5]
     half = aligned(c * 64, 64, 64)
-    pairs = [(sqkv, sheads), (sproject.at[half], srows)]
+    pairs = [(sproject.at[half], srows)]
+    for part in range(3):
+        for j in range(4):
+            column = part * 1024 + j * 256 + lax.div(quarter, 2) * 128
+            pairs.append((sqkv.at[:, aligned(column, 128, 128)], sheads.at[:, pl.ds((part * 4 + j) * 128, 128)]))
     for i in range(2):
         pairs.append((up.at[:, aligned((2 * zl + i) * 512 + quarter * 128, 128, 128)], ups.at[i]))
     pairs.append((down.at[aligned(quarter * 128 + zl * 32, 32, 32)], downs))
@@ -71,13 +75,13 @@
     for copy in start_copies(pairs, sems):
         copy.wait()
 
-    source = lax.broadcasted_iota(jnp.int32, (512, 128), 0)
-    lane = lax.broadcasted_iota(jnp.int32, (512, 128), 1)
-    pick = (source == lane + jnp.where(lane < 64, 0, 192) + quarter * 64).astype(F32).astype(BF)
+    source = lax.broadcasted_iota(jnp.int32, (256, 128), 0)
+    lane = lax.broadcasted_iota(jnp.int32, (256, 128), 1)
+    pick = (source == lane + jnp.where(lane < 64, 0, 64) + c * 64).astype(F32).astype(BF)
     for pair in range(2):
         at = pair * 128
         for part in range(3):
-            block = sheads[:, part * 1024 + pair * 512 : part * 1024 + pair * 512 + 512]
+            block = sheads[:, part * 512 + pair * 256 : part * 512 + pair * 256 + 256]
             got = jnp.dot(block, pick, preferred_element_type=F32).astype(BF)
             for ref in (near, reach):
                 ref[at : at + 128, part * 128 : part * 128 + 128] = got
@@ -91,9 +95,6 @@
     for i in range(4):
         near[320 + i * 32 : 352 + i * 32, 256:512] = downs[:, i * 256 : i * 256 + 256]
 
-    source = lax.broadcasted_iota(jnp.int32, (256, 128), 0)
-    lane = lax.broadcasted_iota(jnp.int32, (256, 128), 1)
-    pick = (source == lane + jnp.where(lane < 64, 0, 64) + c * 64).astype(F32).astype(BF)
     for part in range(3):
         reach[320:448, part * 128 : part * 128 + 128] = jnp.dot(theads[part], pick, preferred_element_type=F32).astype(BF)
     reach[320:384, 384:512] = trows[:, :128]
@@ -107,13 +108,13 @@
         in_specs=[SMEM] + [ANY] * 6,
         out_specs=[VMEM] * 2,
         scratch_shapes=[
-            pltpu.VMEM((128, 3072), BF),
+            pltpu.VMEM((128, 1536), BF),
             pltpu.VMEM((64, 1024), BF),
             pltpu.VMEM((2, 128, 128), BF),
             pltpu.VMEM((32, 1024), BF),
             pltpu.VMEM((3, 128, 256), BF),
             pltpu.VMEM((64, 256), BF),
-            pltpu.SemaphoreType.DMA((9,)),
+            pltpu.SemaphoreType.DMA((20,)),
         ],
         compiler_params=BIG,
         cost_estimate=pl.CostEstimate(flops=120000000, bytes_accessed=2500000, transcendentals=0),
@@ -411,7 +412,8 @@
     own = frames.transpose(1, 0, 2).reshape(ROWS, width)
     far, *near = together(far, *near)
     piece = far[:320]
-    far = far, shift(piece, x=-1), shift(piece, x=2), shift(piece, x=1)
+    far_right = shift(piece, x=-1)
+    far = far, far_right, shift(far_right, x=-1), shift(piece, x=1)
     mlp = stack(near)
     over = swap_chips(own)
     up, down = [mlp, shift(mlp, z=1)], [mlp, shift(mlp, z=-1)]

time: 199 us -> 198 us (level)
  starting transfers between devices: 54.1 us -> 51.2 us
  waiting for transfers between devices: 42.3 us -> 44.5 us
    ppermute x24, starting transfers between devices: 46.4 us -> 43.4 us  [shift(): return lax.ppermute(v, AXES, pairs)]
    ppermute x24, waiting for transfers between devices: 31.5 us -> 34 us  [shift(): return lax.ppermute(v, AXES, pairs)]
  transfers between devices with their start and end apart: 30 -> 30, of which waited for: 15 -> 17; matrix products, arithmetic and copies ran while one was open for 4% -> 4% of each run, Pallas kernels for 9% -> 9%
where the time goes in v1:
time: 198 us; the launch traced here: 197 us
  starting transfers between devices  51.2 us (26%)
  waiting for transfers between devices  44.5 us (22%)
  blocking collectives  40.7 us (21%)
  Pallas kernels  31.3 us (16%)
  between operations  13.8 us (7%)
  local copies, waits for them, and re-layouts  10.4 us (5%)
  other arithmetic  5.48 us (3%)
    ppermute x24, starting transfers between devices, shift(): return lax.ppermute(v, AXES, pairs)  43.4 us
    ppermute x24, waiting for transfers between devices, shift(): return lax.ppermute(v, AXES, pairs)  34 us
    all_to_all x1, blocking collectives, body(): lax.all_to_all(second, AXES, split_axis=0, concat_axis=0, tiled=True, axi...  24.9 us
    all_to_all x1, blocking collectives, body(): lax.all_to_all(done, 'dp', split_axis=0, concat_axis=0, tiled=True)  15.8 us
    ppermute x4, waiting for transfers between devices, swap_chips(): lax.ppermute(v, AXES, [(device(a, b, d, e), device(a, b ^ 1, d, e)) for a...  10.4 us
    pallas_call x1, Pallas kernels, mlp_call(): pl.pallas_call(mlp_kernel, out_shape=[wide(ROWS), wide(2 * ROWS, BF), wid...  7.38 us
    unnamed x62, local copies, waits for them, and re-layouts  7.29 us
    pallas_call x1, Pallas kernels, space_call(): pl.pallas_call(space_kernel, out_shape=[wide(ROWS), wide(2 * ROWS, BF), w...  6.86 us
  transfers between devices with their start and end apart: 30, of which 17 were waited for; matrix products, arithmetic and copies ran while one was open for 4% of the time, Pallas kernels for 9%

profile of v1, /device:TPU:1, one launch (start us, length us, event | category | flops | bytes accessed | tf_op | source)
XLA Modules:
  0.0 197.3 jit_solution(7536745688853314281)
XLA Ops:
  7.1 3.3 %shard_map.100 = (bf16[448,512]{1,0:T(8,128)(2,1)}, bf16[448,512]{1,0:T(8,128)(2,1)}) custom-call(s32[6]{0:T(128)} %stack.27.place, bf16[128,3072]{1,0:T(8,128)(2,1)} %sqkv.1, bf16[128,1024]{1,0:T(8,128)(2,1)} %sproject.1, bf16[128,4096]{1,0:T(8,128)(2,1)} %up.1, bf16[512,1024]{1,0:T(8,128)(2,1)} %down.1, bf16[128,3072]{1,0:T(8,128)(2,1)} %tqkv.1, ...), custom_call_target="tpu_custom_call" | custom-call | flops 120000000 | bytes 2500000 | tf_op jit(solution)/shard_map/pallas_call | solution.py:105
  10.4 3.4 %collective-permute-start.4 = (bf16[448,512]{1,0:T(8,128)(2,1)}, bf16[448,512]{1,0:T(8,128)(2,1)S(1)}, u32[]{:S(2)}, u32[]{:S(2)}) collective-permute-start(bf16[448,512]{1,0:T(8,128)(2,1)} %get-tuple-element.37.a.refs_0_), channel_id=1, source_target_pairs={{0,3},{8,11},{64,67},{72,75},{128,131},{136,139},{192,195},{200,20... | collective-permute-start | bytes 1376264 | tf_op jit(solution)/shard_map/ppermute | solution.py:33
  14.9 6.9 %collective-permute-start.3 = (bf16[448,512]{1,0:T(8,128)(2,1)}, bf16[448,512]{1,0:T(8,128)(2,1)S(1)}, u32[]{:S(2)}, u32[]{:S(2)}) collective-permute-start(bf16[448,512]{1,0:T(8,128)(2,1)} %get-tuple-element.35), channel_id=1, source_target_pairs={{0,4},{8,12},{64,68},{72,76},{128,132},{136,140},{192,196},{200,20... | collective-permute-start | bytes 1376264 | tf_op jit(solution)/shard_map/ppermute | solution.py:33
  22.1 1.9 collective-permute-start
  24.1 0.9 collective-permute-done
  26.1 3.4 %all-to-all-start = ((bf16[8,16,1024]{2,1,0:T(8,128)(2,1)}), bf16[8,16,1024]{2,1,0:T(8,128)(2,1)S(1)}, u32[]{:S(2)}, u32[]{:S(2)}) async-start(bf16[8,16,1024]{2,1,0:T(8,128)(2,1)} %copy.20), calls=%async_computation | async-start | bytes 524288 | tf_op jit(solution)/shard_map/all_to_all | solution.py:411
  29.6 2.8 %collective-permute-done.3.refs_4_ = bf16[448,512]{1,0:T(8,128)(2,1)S(1)} collective-permute-done((bf16[448,512]{1,0:T(8,128)(2,1)}, bf16[448,512]{1,0:T(8,128)(2,1)S(1)}, u32[]{:S(2)}, u32[]{:S(2)}) %collective-permute-start.3) | collective-permute-done | bytes 458784 | tf_op jit(solution)/shard_map/ppermute | solution.py:33
  32.4 5.7 %collective-permute-done.6.d.refs_3_ = bf16[448,512]{1,0:T(8,128)(2,1)S(1)} collective-permute-done((bf16[448,512]{1,0:T(8,128)(2,1)}, bf16[448,512]{1,0:T(8,128)(2,1)S(1)}, u32[]{:S(2)}, u32[]{:S(2)}) %collective-permute-start.6) | collective-permute-done | bytes 458784 | tf_op jit(solution)/shard_map/ppermute | solution.py:33
  39.0 2.0 shard_map.101.refs_0_
  40.9 4.9 %collective-permute-start.7 = (bf16[512,512]{1,0:T(8,128)(2,1)}, bf16[512,512]{1,0:T(8,128)(2,1)S(1)}, u32[]{:S(2)}, u32[]{:S(2)}) collective-permute-start(bf16[512,512]{1,0:T(8,128)(2,1)} %shard_map.101.refs_0_), channel_id=1, source_target_pairs={{0,64},{8,72},{64,128},{72,136},{128,192},{136,200},{192,4},{200,1... | collective-permute-start | bytes 1572872 | tf_op jit(solution)/shard_map/ppermute | solution.py:33
  45.8 0.9 collective-permute-start.8
  47.4 1.9 collective-permute-start.10
  49.5 1.4 collective-permute-start.2
  50.9 0.9 slice.40
  51.8 2.3 %collective-permute-done.11.refs_7_ = bf16[320,512]{1,0:T(8,128)(2,1)S(1)} collective-permute-done((bf16[320,512]{1,0:T(8,128)(2,1)S(1)}, bf16[320,512]{1,0:T(8,128)(2,1)S(1)}, u32[]{:S(2)}, u32[]{:S(2)}) %collective-permute-start.11) | collective-permute-done | bytes 327712 | tf_op jit(solution)/shard_map/ppermute | solution.py:33
  54.1 1.0 collective-permute-done.2.far
  55.2 4.3 %collective-permute-done.8.refs_1_ = bf16[512,512]{1,0:T(8,128)(2,1)S(1)} collective-permute-done((bf16[512,512]{1,0:T(8,128)(2,1)}, bf16[512,512]{1,0:T(8,128)(2,1)S(1)}, u32[]{:S(2)}, u32[]{:S(2)}) %collective-permute-start.8) | collective-permute-done | bytes 524320 | tf_op jit(solution)/shard_map/ppermute | solution.py:33
  60.3 2.4 %collective-permute-start.13 = (bf16[512,512]{1,0:T(8,128)(2,1)S(1)}, bf16[512,512]{1,0:T(8,128)(2,1)S(1)}, u32[]{:S(2)}, u32[]{:S(2)}) collective-permute-start(bf16[512,512]{1,0:T(8,128)(2,1)S(1)} %collective-permute-done.7.refs_7_), channel_id=1, source_target_pairs={{0,64},{8,72},{64,128},{72,136},{128,192},{136,200},{192,4},{200,1... | collective-permute-start | bytes 1572872 | tf_op jit(solution)/shard_map/ppermute | solution.py:33
  62.8 1.5 collective-permute-start.14
  64.2 4.0 %collective-permute-start.1 = (bf16[128,1024]{1,0:T(8,128)(2,1)S(1)}, bf16[128,1024]{1,0:T(8,128)(2,1)S(1)}, u32[]{:S(2)}, u32[]{:S(2)}) collective-permute-start(bf16[128,1024]{1,0:T(8,128)(2,1)S(1)} %bitcast.44), channel_id=1, source_target_pairs={{0,8},{8,0},{64,72},{72,64},{128,136},{136,128},{192,200},{200,192... | collective-permute-start | bytes 786440 | tf_op jit(solution)/shard_map/ppermute | solution.py:33
  68.2 1.2 collective-permute-done.1.other
  70.5 6.9 %shard_map.102 = (f32[128,1024]{1,0:T(8,128)}, bf16[256,1024]{1,0:T(8,128)(2,1)}, f32[128,1024]{1,0:T(8,128)}) custom-call(s32[6]{0:T(128)} %stack.27.place, bf16[128,1024]{1,0:T(8,128)(2,1)} %bitcast.45, bf16[128,1024]{1,0:T(8,128)(2,1)} %copy-done.27, bf16[128,1024]{1,0:T(8,128)(2,1)} %copy-done.21, bf16[128,1024]{1,0:T(8,128)(2,1)} %copy-done.28, ...), custom_call_target="tpu_custom_call" | custom-call | flops 1400000000 | bytes 6000000 | tf_op jit(solution)/shard_map/pallas_call | solution.py:223
  77.9 1.3 collective-permute-start.17
  79.1 2.0 %collective-permute-start.18 = (bf16[512,512]{1,0:T(8,128)(2,1)S(1)}, bf16[512,512]{1,0:T(8,128)(2,1)S(1)}, u32[]{:S(2)}, u32[]{:S(2)}) collective-permute-start(bf16[512,512]{1,0:T(8,128)(2,1)S(1)} %collective-permute-done.14.refs_2_), channel_id=1, source_target_pairs={{0,196},{8,204},{64,0},{72,8},{128,64},{136,72},{192,128},{200,136... | collective-permute-start | bytes 1572872 | tf_op jit(solution)/shard_map/ppermute | solution.py:33
  81.2 1.3 add_convert_fusion.2
  82.5 1.4 collective-permute-start.16
  83.8 9.5 %collective-permute-done.17.refs_5_ = bf16[512,512]{1,0:T(8,128)(2,1)S(1)} collective-permute-done((bf16[512,512]{1,0:T(8,128)(2,1)S(1)}, bf16[512,512]{1,0:T(8,128)(2,1)S(1)}, u32[]{:S(2)}, u32[]{:S(2)}) %collective-permute-start.17) | collective-permute-done | bytes 524320 | tf_op jit(solution)/shard_map/ppermute | solution.py:33
  94.1 2.3 %shard_map.103 = (bf16[128,1024]{1,0:T(8,128)(2,1)}, bf16[128,1024]{1,0:T(8,128)(2,1)}) custom-call(f32[128,1024]{1,0:T(8,128)} %get-tuple-element.47.base, bf16[256,1024]{1,0:T(8,128)(2,1)} %copy-done.4, bf16[128,1024]{1,0:T(8,128)(2,1)} %copy-done.9, f32[1,1024]{1,0:T(1,128)} %bitcast.46), custom_call_target="tpu_custom_call" | custom-call | flops 2000000 | bytes 2500000 | tf_op jit(solution)/shard_map/pallas_call | solution.py:248
  96.4 1.3 collective-permute-start.20
  97.7 1.0 collective-permute-start.19
  99.5 2.0 %collective-permute-start.23 = (bf16[256,512]{1,0:T(8,128)(2,1)S(1)}, bf16[256,512]{1,0:T(8,128)(2,1)S(1)}, u32[]{:S(2)}, u32[]{:S(2)}) collective-permute-start(bf16[256,512]{1,0:T(8,128)(2,1)S(1)} %slice.37), channel_id=1, source_target_pairs={{0,196},{8,204},{64,0},{72,8},{128,64},{136,72},{192,128},{200,136... | collective-permute-start | bytes 786440 | tf_op jit(solution)/shard_map/ppermute | solution.py:33
  101.6 2.1 %collective-permute-done.20.far = bf16[128,1024]{1,0:T(8,128)(2,1)S(1)} collective-permute-done((bf16[128,1024]{1,0:T(8,128)(2,1)}, bf16[128,1024]{1,0:T(8,128)(2,1)S(1)}, u32[]{:S(2)}, u32[]{:S(2)}) %collective-permute-start.20) | collective-permute-done | bytes 262176 | tf_op jit(solution)/shard_map/ppermute | solution.py:37
  103.7 1.9 collective-permute-start.21
  105.6 2.5 %collective-permute-done.22.refs_4_ = bf16[256,512]{1,0:T(8,128)(2,1)S(1)} collective-permute-done((bf16[256,512]{1,0:T(8,128)(2,1)S(1)}, bf16[256,512]{1,0:T(8,128)(2,1)S(1)}, u32[]{:S(2)}, u32[]{:S(2)}) %collective-permute-start.22) | collective-permute-done | bytes 262176 | tf_op jit(solution)/shard_map/ppermute | solution.py:33
  109.2 7.4 %shard_map.104 = (f32[128,1024]{1,0:T(8,128)}, bf16[256,1024]{1,0:T(8,128)(2,1)}, f32[128,1024]{1,0:T(8,128)}) custom-call(s32[6]{0:T(128)} %stack.27.place, bf16[128,1024]{1,0:T(8,128)(2,1)} %get-tuple-element.56.first, bf16[128,1024]{1,0:T(8,128)(2,1)} %get-tuple-element.57.own, bf16[128,1024]{1,0:T(8,128)(2,1)} %copy-done.23, ...), custom_call_target="tpu_custom_call" | custom-call | flops 2200000000 | bytes 9000000 | tf_op jit(solution)/shard_map/pallas_call | solution.py:293
  117.4 1.7 collective-permute-done.24
  119.1 1.1 add_convert_fusion.1
  120.5 7.3 %collective-permute-done.25 = bf16[128,1024]{1,0:T(8,128)(2,1)S(1)} collective-permute-done((bf16[128,1024]{1,0:T(8,128)(2,1)S(1)}, bf16[128,1024]{1,0:T(8,128)(2,1)S(1)}, u32[]{:S(2)}, u32[]{:S(2)}) %collective-permute-start.25) | collective-permute-done | bytes 262176 | tf_op jit(solution)/shard_map/ppermute | solution.py:37
  127.8 1.1 fusion
  130.4 24.9 %all_to_all.21 = bf16[128,2,512]{2,1,0:T(2,128)(2,1)S(1)} all-to-all(bf16[128,2,512]{2,1,0:T(2,128)(2,1)S(1)} %reshape.30), channel_id=1, replica_groups={{0,1,2,3,4,5,6,7,16,17,18,19,20,21,22,23,32,33,34,35,36,37,38,39,48,49,..., dimensions={0} | all-to-all | bytes 524288 | tf_op jit(solution)/shard_map/all_to_all | solution.py:445
  155.7 3.0 %collective-permute-start.26 = (bf16[128,1024]{1,0:T(8,128)(2,1)S(1)}, bf16[128,1024]{1,0:T(8,128)(2,1)S(1)}, u32[]{:S(2)}, u32[]{:S(2)}) collective-permute-start(bf16[128,1024]{1,0:T(8,128)(2,1)S(1)} %bitcast.36), channel_id=1, source_target_pairs={{0,8},{8,0},{64,72},{72,64},{128,136},{136,128},{192,200},{200,192... | collective-permute-start | bytes 786440 | tf_op jit(solution)/shard_map/ppermute | solution.py:33
  158.7 1.2 collective-permute-done.26.other
  159.9 2.2 %copy-done.2 = bf16[4096,512]{1,0:T(8,128)(2,1)S(1)} copy-done((bf16[4096,512]{1,0:T(8,128)(2,1)S(1)}, bf16[4096,512]{1,0:T(8,128)(2,1)}, u32[]{:S(2)}) %copy-start.2) | copy-done | bytes 4194328
  162.1 5.7 %shard_map.105 = (f32[128,1024]{1,0:T(8,128)S(1)}, bf16[128,1024]{1,0:T(8,128)(2,1)S(1)}) custom-call(s32[6]{0:T(128)S(1)} %copy-done.1, bf16[128,1024]{1,0:T(8,128)(2,1)S(1)} %bitcast.37, bf16[128,1024]{1,0:T(8,128)(2,1)S(1)} %collective-permute-done.26.other, f32[1,1024]{1,0:T(1,128)S(1)} %bitcast.38, bf16[4096,512]{1,0:T(8,128)(2,1)S(1)} %copy-done.2), custom_call_target="tpu_custom_call" | custom-call | flops 1400000000 | bytes 6000000 | tf_op jit(solution)/shard_map/pallas_call | solution.py:341
  169.0 1.2 collective-permute-done.27.came
  170.9 1.9 shard_map.106
  172.8 15.8 %all_to_all.22.came = bf16[32,8,512]{2,1,0:T(8,128)(2,1)} all-to-all(bf16[32,8,512]{2,1,0:T(8,128)(2,1)} %bitcast.42), channel_id=1, replica_groups=mesh['dp'=32,'fsdp'=8] {'dp'}, dimensions={0} | all-to-all | bytes 524288 | tf_op jit(solution)/shard_map/all_to_all | solution.py:448
  188.6 1.9 shard_map.107
  (102 shorter events, 14.8 us)
Async XLA Ops:
  6.5 15.3 %copy-start.10 = (bf16[1,4,32,1024]{3,2,1,0:T(8,128)(2,1)S(1)}, bf16[1,4,32,1024]{3,2,1,0:T(8,128)(2,1)}, u32[]{:S(2)}) copy-start(bf16[1,4,32,1024]{3,2,1,0:T(8,128)(2,1)} %param.10) | copy-start | bytes 786436
  10.4 22.0 %collective-permute-start.4 = (bf16[448,512]{1,0:T(8,128)(2,1)}, bf16[448,512]{1,0:T(8,128)(2,1)S(1)}, u32[]{:S(2)}, u32[]{:S(2)}) collective-permute-start(bf16[448,512]{1,0:T(8,128)(2,1)} %get-tuple-element.37.a.refs_0_), channel_id=1, source_target_pairs={{0,3},{8,11},{64,67},{72,75},{128,131},{136,139},{192,195},{200,20... | collective-permute-start | bytes 1376264 | tf_op jit(solution)/shard_map/ppermute | solution.py:33
  13.8 18.6 %collective-permute-start.5 = (bf16[448,512]{1,0:T(8,128)(2,1)}, bf16[448,512]{1,0:T(8,128)(2,1)S(1)}, u32[]{:S(2)}, u32[]{:S(2)}) collective-permute-start(bf16[448,512]{1,0:T(8,128)(2,1)} %get-tuple-element.37.a.refs_0_), channel_id=1, source_target_pairs={{0,2},{8,10},{64,66},{72,74},{128,130},{136,138},{192,194},{200,20... | collective-permute-start | bytes 1376264 | tf_op jit(solution)/shard_map/ppermute | solution.py:33
  14.3 23.8 %collective-permute-start.6 = (bf16[448,512]{1,0:T(8,128)(2,1)}, bf16[448,512]{1,0:T(8,128)(2,1)S(1)}, u32[]{:S(2)}, u32[]{:S(2)}) collective-permute-start(bf16[448,512]{1,0:T(8,128)(2,1)} %get-tuple-element.37.a.refs_0_), channel_id=1, source_target_pairs={{0,1},{8,9},{64,65},{72,73},{128,129},{136,137},{192,193},{200,201... | collective-permute-start | bytes 1376264 | tf_op jit(solution)/shard_map/ppermute | solution.py:33
  14.9 17.5 %collective-permute-start.3 = (bf16[448,512]{1,0:T(8,128)(2,1)}, bf16[448,512]{1,0:T(8,128)(2,1)S(1)}, u32[]{:S(2)}, u32[]{:S(2)}) collective-permute-start(bf16[448,512]{1,0:T(8,128)(2,1)} %get-tuple-element.35), channel_id=1, source_target_pairs={{0,4},{8,12},{64,68},{72,76},{128,132},{136,140},{192,196},{200,20... | collective-permute-start | bytes 1376264 | tf_op jit(solution)/shard_map/ppermute | solution.py:33
  22.1 2.9 %collective-permute-start = (bf16[4,16,1024]{2,0,1:T(4,128)(2,1)S(1)}, bf16[4,16,1024]{2,0,1:T(4,128)(2,1)S(1)}, u32[]{:S(2)}, u32[]{:S(2)}) collective-permute-start(bf16[4,16,1024]{2,0,1:T(4,128)(2,1)S(1)} %fusion.1), channel_id=1, source_target_pairs={{0,8},{8,0},{64,72},{72,64},{128,136},{136,128},{192,200},{200,192... | collective-permute-start | bytes 393224 | tf_op jit(solution)/shard_map/ppermute | solution.py:33
  26.1 23.3 %all-to-all-start = ((bf16[8,16,1024]{2,1,0:T(8,128)(2,1)}), bf16[8,16,1024]{2,1,0:T(8,128)(2,1)S(1)}, u32[]{:S(2)}, u32[]{:S(2)}) async-start(bf16[8,16,1024]{2,1,0:T(8,128)(2,1)} %copy.20), calls=%async_computation | async-start | bytes 524288 | tf_op jit(solution)/shard_map/all_to_all | solution.py:411
  29.5 130.4 %all-gather.2.cloned.1.call-start = ((), (), s32[]{:S(2)}) async-start(), calls=%async_computation.3 | async-start | bytes 4456448 | tf_op jit(solution)/shard_map/all_gather | solution.py:425
  32.4 37.4 %copy-start.8 = (bf16[448,512]{1,0:T(8,128)(2,1)}, bf16[448,512]{1,0:T(8,128)(2,1)S(1)}, u32[]{:S(2)}) copy-start(bf16[448,512]{1,0:T(8,128)(2,1)S(1)} %collective-permute-done.3.refs_4_) | copy-start | bytes 1376260
  32.4 5.9 %copy-start.5 = (bf16[448,512]{1,0:T(8,128)(2,1)}, bf16[448,512]{1,0:T(8,128)(2,1)S(1)}, u32[]{:S(2)}) copy-start(bf16[448,512]{1,0:T(8,128)(2,1)S(1)} %collective-permute-done.4.b.refs_1_) | copy-start | bytes 1376260
  32.4 5.9 %copy-start.6 = (bf16[448,512]{1,0:T(8,128)(2,1)}, bf16[448,512]{1,0:T(8,128)(2,1)S(1)}, u32[]{:S(2)}) copy-start(bf16[448,512]{1,0:T(8,128)(2,1)S(1)} %collective-permute-done.5.c.refs_2_) | copy-start | bytes 1376260
  38.2 9.3 %collective-permute-start.9 = (bf16[320,512]{1,0:T(8,128)(2,1)S(1)}, bf16[320,512]{1,0:T(8,128)(2,1)}, u32[]{:S(2)}, u32[]{:S(2)}) collective-permute-start(bf16[320,512]{1,0:T(8,128)(2,1)S(1)} %slice.34), channel_id=1, source_target_pairs={{0,3},{8,11},{64,67},{72,75},{128,131},{136,139},{192,195},{200,20... | collective-permute-start | bytes 983048 | tf_op jit(solution)/shard_map/ppermute | solution.py:33
  40.9 14.3 %collective-permute-start.7 = (bf16[512,512]{1,0:T(8,128)(2,1)}, bf16[512,512]{1,0:T(8,128)(2,1)S(1)}, u32[]{:S(2)}, u32[]{:S(2)}) collective-permute-start(bf16[512,512]{1,0:T(8,128)(2,1)} %shard_map.101.refs_0_), channel_id=1, source_target_pairs={{0,64},{8,72},{64,128},{72,136},{128,192},{136,200},{192,4},{200,1... | collective-permute-start | bytes 1572872 | tf_op jit(solution)/shard_map/ppermute | solution.py:33
  45.8 13.7 %collective-permute-start.8 = (bf16[512,512]{1,0:T(8,128)(2,1)}, bf16[512,512]{1,0:T(8,128)(2,1)S(1)}, u32[]{:S(2)}, u32[]{:S(2)}) collective-permute-start(bf16[512,512]{1,0:T(8,128)(2,1)} %shard_map.101.refs_0_), channel_id=1, source_target_pairs={{0,196},{8,204},{64,0},{72,8},{128,64},{136,72},{192,128},{200,136... | collective-permute-start | bytes 1572872 | tf_op jit(solution)/shard_map/ppermute | solution.py:33
  46.7 7.4 %collective-permute-start.11 = (bf16[320,512]{1,0:T(8,128)(2,1)S(1)}, bf16[320,512]{1,0:T(8,128)(2,1)S(1)}, u32[]{:S(2)}, u32[]{:S(2)}) collective-permute-start(bf16[320,512]{1,0:T(8,128)(2,1)S(1)} %slice.34), channel_id=1, source_target_pairs={{0,1},{8,9},{64,65},{72,73},{128,129},{136,137},{192,193},{200,201... | collective-permute-start | bytes 983048 | tf_op jit(solution)/shard_map/ppermute | solution.py:33
  47.4 12.1 %collective-permute-start.10 = (bf16[320,512]{1,0:T(8,128)(2,1)}, bf16[320,512]{1,0:T(8,128)(2,1)S(1)}, u32[]{:S(2)}, u32[]{:S(2)}) collective-permute-start(bf16[320,512]{1,0:T(8,128)(2,1)} %collective-permute-done.9.refs_5_), channel_id=1, source_target_pairs={{0,3},{8,11},{64,67},{72,75},{128,131},{136,139},{192,195},{200,20... | collective-permute-start | bytes 983048 | tf_op jit(solution)/shard_map/ppermute | solution.py:33
  49.5 20.3 %copy-start.11 = (bf16[16,8,1024]{2,1,0:T(8,128)(2,1)}, bf16[16,8,1024]{2,1,0:T(8,128)(2,1)S(1)}, u32[]{:S(2)}) copy-start(bf16[16,8,1024]{2,1,0:T(8,128)(2,1)S(1)} %copy.28) | copy-start | bytes 786436
  49.5 5.6 %collective-permute-start.2 = (bf16[128,1024]{1,0:T(8,128)(2,1)S(1)}, bf16[128,1024]{1,0:T(8,128)(2,1)S(1)}, u32[]{:S(2)}, u32[]{:S(2)}) collective-permute-start(bf16[128,1024]{1,0:T(8,128)(2,1)S(1)} %bitcast.43), channel_id=1, source_target_pairs={{0,16},{8,24},{64,80},{72,88},{128,144},{136,152},{192,208},{200,2... | collective-permute-start | bytes 786440 | tf_op jit(solution)/shard_map/ppermute | solution.py:37
  54.1 15.7 %copy-start.19 = (bf16[320,512]{1,0:T(8,128)(2,1)}, bf16[320,512]{1,0:T(8,128)(2,1)S(1)}, u32[]{:S(2)}) copy-start(bf16[320,512]{1,0:T(8,128)(2,1)S(1)} %collective-permute-done.11.refs_7_) | copy-start | bytes 983044
  55.1 14.7 %copy-start.21 = (bf16[128,1024]{1,0:T(8,128)(2,1)}, bf16[128,1024]{1,0:T(8,128)(2,1)S(1)}, u32[]{:S(2)}) copy-start(bf16[128,1024]{1,0:T(8,128)(2,1)S(1)} %collective-permute-done.2.far) | copy-start | bytes 786436
  55.2 41.2 %copy-start.15 = (bf16[512,512]{1,0:T(8,128)(2,1)}, bf16[512,512]{1,0:T(8,128)(2,1)S(1)}, u32[]{:S(2)}) copy-start(bf16[512,512]{1,0:T(8,128)(2,1)S(1)} %collective-permute-done.7.refs_7_) | copy-start | bytes 1572868
  59.5 36.9 %copy-start.16 = (bf16[512,512]{1,0:T(8,128)(2,1)}, bf16[512,512]{1,0:T(8,128)(2,1)S(1)}, u32[]{:S(2)}) copy-start(bf16[512,512]{1,0:T(8,128)(2,1)S(1)} %collective-permute-done.8.refs_1_) | copy-start | bytes 1572868
  59.5 10.3 %copy-start.20 = (bf16[320,512]{1,0:T(8,128)(2,1)}, bf16[320,512]{1,0:T(8,128)(2,1)S(1)}, u32[]{:S(2)}) copy-start(bf16[320,512]{1,0:T(8,128)(2,1)S(1)} %collective-permute-done.10.refs_6_) | copy-start | bytes 983044
  60.3 17.0 %collective-permute-start.13 = (bf16[512,512]{1,0:T(8,128)(2,1)S(1)}, bf16[512,512]{1,0:T(8,128)(2,1)S(1)}, u32[]{:S(2)}, u32[]{:S(2)}) collective-permute-start(bf16[512,512]{1,0:T(8,128)(2,1)S(1)} %collective-permute-done.7.refs_7_), channel_id=1, source_target_pairs={{0,64},{8,72},{64,128},{72,136},{128,192},{136,200},{192,4},{200,1... | collective-permute-start | bytes 1572872 | tf_op jit(solution)/shard_map/ppermute | solution.py:33
  62.8 14.6 %collective-permute-start.14 = (bf16[512,512]{1,0:T(8,128)(2,1)S(1)}, bf16[512,512]{1,0:T(8,128)(2,1)S(1)}, u32[]{:S(2)}, u32[]{:S(2)}) collective-permute-start(bf16[512,512]{1,0:T(8,128)(2,1)S(1)} %collective-permute-done.8.refs_1_), channel_id=1, source_target_pairs={{0,196},{8,204},{64,0},{72,8},{128,64},{136,72},{192,128},{200,136... | collective-permute-start | bytes 1572872 | tf_op jit(solution)/shard_map/ppermute | solution.py:33
  64.2 5.2 %collective-permute-start.1 = (bf16[128,1024]{1,0:T(8,128)(2,1)S(1)}, bf16[128,1024]{1,0:T(8,128)(2,1)S(1)}, u32[]{:S(2)}, u32[]{:S(2)}) collective-permute-start(bf16[128,1024]{1,0:T(8,128)(2,1)S(1)} %bitcast.44), channel_id=1, source_target_pairs={{0,8},{8,0},{64,72},{72,64},{128,136},{136,128},{192,200},{200,192... | collective-permute-start | bytes 786440 | tf_op jit(solution)/shard_map/ppermute | solution.py:33
  68.2 1.5 collective-permute-start.12
  77.4 16.0 %copy-start.17 = (bf16[512,512]{1,0:T(8,128)(2,1)}, bf16[512,512]{1,0:T(8,128)(2,1)S(1)}, u32[]{:S(2)}) copy-start(bf16[512,512]{1,0:T(8,128)(2,1)S(1)} %collective-permute-done.13.refs_6_) | copy-start | bytes 1572868
  77.4 16.0 %copy-start.18 = (bf16[512,512]{1,0:T(8,128)(2,1)}, bf16[512,512]{1,0:T(8,128)(2,1)S(1)}, u32[]{:S(2)}) copy-start(bf16[512,512]{1,0:T(8,128)(2,1)S(1)} %collective-permute-done.14.refs_2_) | copy-start | bytes 1572868
  77.4 3.8 %collective-permute-start.15 = (bf16[256,1024]{1,0:T(8,128)(2,1)}, bf16[256,1024]{1,0:T(8,128)(2,1)S(1)}, u32[]{:S(2)}, u32[]{:S(2)}) collective-permute-start(bf16[256,1024]{1,0:T(8,128)(2,1)} %get-tuple-element.51), channel_id=1, source_target_pairs={{0,8},{8,0},{64,72},{72,64},{128,136},{136,128},{192,200},{200,192... | collective-permute-start | bytes 1572872 | tf_op jit(solution)/shard_map/ppermute | solution.py:33
  77.9 15.5 %collective-permute-start.17 = (bf16[512,512]{1,0:T(8,128)(2,1)S(1)}, bf16[512,512]{1,0:T(8,128)(2,1)S(1)}, u32[]{:S(2)}, u32[]{:S(2)}) collective-permute-start(bf16[512,512]{1,0:T(8,128)(2,1)S(1)} %collective-permute-done.13.refs_6_), channel_id=1, source_target_pairs={{0,64},{8,72},{64,128},{72,136},{128,192},{136,200},{192,4},{200,1... | collective-permute-start | bytes 1572872 | tf_op jit(solution)/shard_map/ppermute | solution.py:33
  79.1 14.2 %collective-permute-start.18 = (bf16[512,512]{1,0:T(8,128)(2,1)S(1)}, bf16[512,512]{1,0:T(8,128)(2,1)S(1)}, u32[]{:S(2)}, u32[]{:S(2)}) collective-permute-start(bf16[512,512]{1,0:T(8,128)(2,1)S(1)} %collective-permute-done.14.refs_2_), channel_id=1, source_target_pairs={{0,196},{8,204},{64,0},{72,8},{128,64},{136,72},{192,128},{200,136... | collective-permute-start | bytes 1572872 | tf_op jit(solution)/shard_map/ppermute | solution.py:33
  81.2 12.2 %copy-start.4 = (bf16[256,1024]{1,0:T(8,128)(2,1)}, bf16[256,1024]{1,0:T(8,128)(2,1)S(1)}, u32[]{:S(2)}) copy-start(bf16[256,1024]{1,0:T(8,128)(2,1)S(1)} %collective-permute-done.15.came) | copy-start | bytes 1572868
  82.5 10.9 %collective-permute-start.16 = (bf16[128,1024]{1,0:T(8,128)(2,1)S(1)}, bf16[128,1024]{1,0:T(8,128)(2,1)S(1)}, u32[]{:S(2)}, u32[]{:S(2)}) collective-permute-start(bf16[128,1024]{1,0:T(8,128)(2,1)S(1)} %add_convert_fusion.2), channel_id=1, source_target_pairs={{0,16},{8,24},{64,80},{72,88},{128,144},{136,152},{192,208},{200,2... | collective-permute-start | bytes 786440 | tf_op jit(solution)/shard_map/ppermute | solution.py:37
  93.3 15.1 %copy-start.13 = (bf16[512,512]{1,0:T(8,128)(2,1)}, bf16[512,512]{1,0:T(8,128)(2,1)S(1)}, u32[]{:S(2)}) copy-start(bf16[512,512]{1,0:T(8,128)(2,1)S(1)} %collective-permute-done.17.refs_5_) | copy-start | bytes 1572868
  93.3 15.1 %copy-start.14 = (bf16[512,512]{1,0:T(8,128)(2,1)}, bf16[512,512]{1,0:T(8,128)(2,1)S(1)}, u32[]{:S(2)}) copy-start(bf16[512,512]{1,0:T(8,128)(2,1)S(1)} %collective-permute-done.18.refs_3_) | copy-start | bytes 1572868
  96.4 7.3 %collective-permute-start.20 = (bf16[128,1024]{1,0:T(8,128)(2,1)}, bf16[128,1024]{1,0:T(8,128)(2,1)S(1)}, u32[]{:S(2)}, u32[]{:S(2)}) collective-permute-start(bf16[128,1024]{1,0:T(8,128)(2,1)} %get-tuple-element.57.own), channel_id=1, source_target_pairs={{0,16},{8,24},{64,80},{72,88},{128,144},{136,152},{192,208},{200,2... | collective-permute-start | bytes 786440 | tf_op jit(solution)/shard_map/ppermute | solution.py:37
  97.7 7.9 %collective-permute-start.19 = (bf16[128,1024]{1,0:T(8,128)(2,1)}, bf16[128,1024]{1,0:T(8,128)(2,1)S(1)}, u32[]{:S(2)}, u32[]{:S(2)}) collective-permute-start(bf16[128,1024]{1,0:T(8,128)(2,1)} %get-tuple-element.57.own), channel_id=1, source_target_pairs={{0,8},{8,0},{64,72},{72,64},{128,136},{136,128},{192,200},{200,192... | collective-permute-start | bytes 786440 | tf_op jit(solution)/shard_map/ppermute | solution.py:33
  98.7 9.3 %collective-permute-start.22 = (bf16[256,512]{1,0:T(8,128)(2,1)S(1)}, bf16[256,512]{1,0:T(8,128)(2,1)S(1)}, u32[]{:S(2)}, u32[]{:S(2)}) collective-permute-start(bf16[256,512]{1,0:T(8,128)(2,1)S(1)} %slice.36), channel_id=1, source_target_pairs={{0,64},{8,72},{64,128},{72,136},{128,192},{136,200},{192,4},{200,1... | collective-permute-start | bytes 786440 | tf_op jit(solution)/shard_map/ppermute | solution.py:33
  99.5 8.8 %collective-permute-start.23 = (bf16[256,512]{1,0:T(8,128)(2,1)S(1)}, bf16[256,512]{1,0:T(8,128)(2,1)S(1)}, u32[]{:S(2)}, u32[]{:S(2)}) collective-permute-start(bf16[256,512]{1,0:T(8,128)(2,1)S(1)} %slice.37), channel_id=1, source_target_pairs={{0,196},{8,204},{64,0},{72,8},{128,64},{136,72},{192,128},{200,136... | collective-permute-start | bytes 786440 | tf_op jit(solution)/shard_map/ppermute | solution.py:33
  103.7 4.7 %copy-start.22 = (bf16[128,1024]{1,0:T(8,128)(2,1)}, bf16[128,1024]{1,0:T(8,128)(2,1)S(1)}, u32[]{:S(2)}) copy-start(bf16[128,1024]{1,0:T(8,128)(2,1)S(1)} %collective-permute-done.20.far) | copy-start | bytes 786436
  103.7 4.7 %collective-permute-start.21 = (bf16[128,1024]{1,0:T(8,128)(2,1)S(1)}, bf16[128,1024]{1,0:T(8,128)(2,1)S(1)}, u32[]{:S(2)}, u32[]{:S(2)}) collective-permute-start(bf16[128,1024]{1,0:T(8,128)(2,1)S(1)} %collective-permute-done.20.far), channel_id=1, source_target_pairs={{0,8},{8,0},{64,72},{72,64},{128,136},{136,128},{192,200},{200,192... | collective-permute-start | bytes 786440 | tf_op jit(solution)/shard_map/ppermute | solution.py:33
  116.6 43.3 %copy-start.1 = (s32[6]{0:T(128)S(1)}, s32[6]{0:T(128)}, u32[]{:S(2)}) copy-start(s32[6]{0:T(128)} %stack.27.place) | copy-start | bytes 76
  116.6 43.3 %copy-start.3 = (f32[1024]{0:T(1024)S(1)}, f32[1024]{0:T(1024)}, u32[]{:S(2)}) copy-start(f32[1024]{0:T(1024)} %param.17) | copy-start | bytes 12292
  116.6 2.5 %collective-permute-start.24 = (bf16[256,1024]{1,0:T(8,128)(2,1)}, bf16[256,1024]{1,0:T(8,128)(2,1)S(1)}, u32[]{:S(2)}, u32[]{:S(2)}) collective-permute-start(bf16[256,1024]{1,0:T(8,128)(2,1)} %get-tuple-element.61), channel_id=1, source_target_pairs={{0,8},{8,0},{64,72},{72,64},{128,136},{136,128},{192,200},{200,192... | collective-permute-start | bytes 1572872 | tf_op jit(solution)/shard_map/ppermute | solution.py:33
  120.2 7.6 %collective-permute-start.25 = (bf16[128,1024]{1,0:T(8,128)(2,1)S(1)}, bf16[128,1024]{1,0:T(8,128)(2,1)S(1)}, u32[]{:S(2)}, u32[]{:S(2)}) collective-permute-start(bf16[128,1024]{1,0:T(8,128)(2,1)S(1)} %add_convert_fusion.1), channel_id=1, source_target_pairs={{0,16},{8,24},{64,80},{72,88},{128,144},{136,152},{192,208},{200,2... | collective-permute-start | bytes 786440 | tf_op jit(solution)/shard_map/ppermute | solution.py:37
  155.7 4.2 %collective-permute-start.26 = (bf16[128,1024]{1,0:T(8,128)(2,1)S(1)}, bf16[128,1024]{1,0:T(8,128)(2,1)S(1)}, u32[]{:S(2)}, u32[]{:S(2)}) collective-permute-start(bf16[128,1024]{1,0:T(8,128)(2,1)S(1)} %bitcast.36), channel_id=1, source_target_pairs={{0,8},{8,0},{64,72},{72,64},{128,136},{136,128},{192,200},{200,192... | collective-permute-start | bytes 786440 | tf_op jit(solution)/shard_map/ppermute | solution.py:33
  168.6 1.5 collective-permute-start.27
  (11 other events, 11.7 us)
Sparse Core Ops, SparseCore 0:
  60.5 63.3 all-gather.1
